TPU v7x, 256 devices: a whole 4x4x8 slice. The times are simulated.
256 devices in a mesh: bunch: 16 (over x, y), mp: 16 (over z, core).
Axes of the slice: x: 4, y: 4, z: 8, core: 2. Of those that a mesh axis runs over, the one named last changes fastest.
Arguments:
- phase_space: float32 [4, 256, 65536], P(None, 'bunch', 'mp')
- phase_advance: float32 [2, 256], P(None, 'bunch'), may hold values from 0.3 to 2.8
- centroid_history: float32 [2, 64, 256], P(None, None, 'bunch'), may hold values from -6 to 6
- lr_wake: float32 [16640], replicated, may hold values from -0.046875 to 0.046875
- sr_dipole: float32 [256, 256], replicated, may hold values from -24 to 24
- sr_quad: float32 [256, 256], replicated, may hold values from -24 to 24
- slice_ids: int32 [2, 256, 65536], P(None, 'bunch', 'mp'), may hold values from 0 to 255
Outputs:
- tracked: float32 [4, 256, 65536], P(None, 'bunch', 'mp')
- centroids: float32 [2, 2, 256], P(None, None, 'bunch')
All inputs are finite; a program needn't handle non-finite values.
Results may differ from a plain program's by a relative error of at most 0.00019.
Values sent between devices are 32-bit elements; how exact they have to be, the bound alone decides.
A program may use at most 64 MiB of HBM per device.

v0:
```python
import jax
import jax.numpy as jnp
from jax import lax
from jax.sharding import PartitionSpec as P

SLICES = 256
TURNS = 2


DETUNE = 0.02


def sent_to_all(array, axis):
    copies = jnp.broadcast_to(array, (lax.axis_size(axis), *array.shape))
    return lax.all_to_all(copies, axis, split_axis=0, concat_axis=0, tiled=True)


def over_copies(array, axis):
    everything = sent_to_all(array, axis)
    return jnp.sum(everything, axis=0)


def gather_turned(arrays, axis, dims):
    turned = [jnp.moveaxis(a, dim, 0) for a, dim in zip(arrays, dims)]
    widths = [t[0].size for t in turned]
    both = jnp.concatenate([t.reshape(-1, w) for t, w in zip(turned, widths)], axis=1)
    whole = lax.all_gather(both, axis, axis=0, tiled=True)
    tiles = jnp.split(whole, [sum(widths[:k]) for k in range(1, len(widths))], axis=1)
    return tuple(
        (
            jnp.moveaxis(b.reshape(-1, *t.shape[1:]), 0, dim)
            for b, t, dim in zip(tiles, turned, dims)
        )
    )


def body(phase_space, phase_advance, centroid_history, lr_wake, sr_dipole, sr_quad, slice_ids):
    highest = lax.Precision.HIGHEST
    bunch_dev = phase_space.shape[1]
    depth = centroid_history.shape[1]
    macro_total = phase_space.shape[2] * lax.axis_size("mp")
    all_bunches = bunch_dev * lax.axis_size("bunch")
    length = (depth + 1) * all_bunches
    offset_bunch = lax.axis_index("bunch") * bunch_dev
    own_index = jnp.arange(bunch_dev, dtype=jnp.int32)
    levels = jnp.arange(SLICES, dtype=jnp.int32)
    padded = jnp.concatenate([jnp.zeros((all_bunches,), jnp.float32), lr_wake])
    windows = jax.vmap(lambda start_at: lax.dynamic_slice(padded, (start_at,), (length,)))(
        offset_bunch + own_index
    )
    history = centroid_history

    def moments_of(member):
        slice_line, line_x, line_y = member
        onehot = (slice_line[:, None] == levels[None, :]).astype(jnp.float32)
        stacked = jnp.stack([jnp.ones_like(line_x), line_x, line_y])
        return jnp.dot(stacked, onehot, precision=highest, preferred_element_type=jnp.float32)

    def lookup(member):
        slice_line, kick_rows = member
        onehot = (slice_line[:, None] == levels[None, :]).astype(jnp.float32)
        return lax.dot_general(
            kick_rows,
            onehot,
            (((1,), (1,)), ((), ())),
            precision=highest,
            preferred_element_type=jnp.float32,
        )

    coords = phase_space
    centroid_rows = []
    for turn_index in range(TURNS):
        slice_row = slice_ids[turn_index]
        moments = lax.map(moments_of, (slice_row, coords[0], coords[2]))
        moments = over_copies(moments, "mp")
        density = moments[:, 0] / macro_total
        dipole = jnp.stack([moments[:, 1], moments[:, 2]]) / macro_total
        centroid = jnp.sum(dipole, axis=2)
        centroid_rows.append(centroid)
        dip_kick = jnp.einsum("pbj,ij->pbi", dipole, sr_dipole, precision=highest)
        quad_kick = jnp.einsum("bj,ij->bi", density, sr_quad, precision=highest)
        whole_past, current_all = gather_turned((history, centroid), "bunch", (2, 1))
        all_rows = jnp.concatenate([current_all[:, None, :], whole_past], axis=1)[
            :, :, ::-1
        ].reshape(2, length)
        far_kick = jnp.einsum("bk,pk->pb", windows, all_rows, precision=highest)
        kick_table = jnp.stack([dip_kick[0], dip_kick[1], quad_kick], axis=1)
        picked = lax.map(lookup, (slice_row, kick_table))
        coord_x, moment_x, coord_y, moment_y = (coords[0], coords[1], coords[2], coords[3])
        moment_x = moment_x + picked[:, 0] + picked[:, 2] * coord_x + far_kick[0][:, None]
        moment_y = moment_y + picked[:, 1] - picked[:, 2] * coord_y + far_kick[1][:, None]
        action = coord_x * coord_x + moment_x * moment_x + coord_y * coord_y + moment_y * moment_y
        angle_x = phase_advance[0][:, None] + DETUNE * action
        angle_y = phase_advance[1][:, None] + DETUNE * action
        new_x = jnp.cos(angle_x) * coord_x + jnp.sin(angle_x) * moment_x
        new_mx = -jnp.sin(angle_x) * coord_x + jnp.cos(angle_x) * moment_x
        new_y = jnp.cos(angle_y) * coord_y + jnp.sin(angle_y) * moment_y
        new_my = -jnp.sin(angle_y) * coord_y + jnp.cos(angle_y) * moment_y
        coords = jnp.stack([new_x, new_mx, new_y, new_my])
        history = jnp.concatenate([centroid[:, None, :], history[:, :-1]], axis=1)
    return (coords, jnp.stack(centroid_rows, axis=1))


def solution(mesh):
    placed = (
        P(None, "bunch", "mp"),
        P(None, "bunch"),
        P(None, None, "bunch"),
        P(),
        P(),
        P(),
        P(None, "bunch", "mp"),
    )
    return jax.shard_map(
        body,
        mesh=mesh,
        in_specs=placed,
        out_specs=(P(None, "bunch", "mp"), P(None, None, "bunch")),
        check_vma=False,
    )
```

profile of v0, /device:TPU:1, one launch (start us, length us, event | category | flops | bytes accessed | tf_op | source)
XLA Modules:
  0.0 321.7 jit_solution(3574766325816593291)
XLA Ops:
  1.9 25.5 %while.46 = (s32[]{:T(128)}, f32[16,3,256]{2,0,1:T(8,128)S(1)}, f32[16,4096]{1,0:T(8,128)S(1)}, f32[16,4096]{1,0:T(8,128)S(1)}, s32[16,4096]{1,0:T(8,128)S(1)}, ...) while((s32[]{:T(128)}, f32[16,3,256]{2,0,1:T(8,128)S(1)}, f32[16,4096]{1,0:T(8,128)S(1)}, ...), condition=%wide.region_1.2_spmd.clone, body=%wide.region_0.1_spmd.clone.sunk | while | flops 38821888 | bytes 162961 | solution.py:74
  28.5 10.0 %all-to-all-start = ((f32[16,16,3,256]{3,1,2,0:T(8,128)}), f32[16,16,3,256]{3,1,2,0:T(8,128)S(1)}, u32[]{:S(2)}, u32[]{:S(2)}) async-start(f32[16,16,3,256]{3,1,2,0:T(8,128)} %broadcast_in_dim.39), calls=%async_computation | async-start | bytes 1572864 | tf_op jit(solution)/shard_map/all_to_all | solution.py:15
  38.6 36.2 %while.45 = (s32[]{:T(128)}, f32[16896]{0:T(1024)S(1)}, s32[16,1]{0,1:T(1,128)S(1)}, f32[16,16640]{1,0:T(8,128)S(1)}, s32[]{:T(128)}, /*index=5*/s32[]{:T(128)}) while((s32[]{:T(128)}, f32[16896]{0:T(1024)S(1)}, s32[16,1]{0,1:T(1,128)S(1)}, f32[16,16640]{1,0:T(8,128)S(1)}, s32[]{:T(128)}, /*index=5*/s32[]{:T(128)}) %tuple.122), condition=%wide.while_cond, body=%wide.while_body.sunk | while | flops 2 | bytes 399457 | solution.py:48
  75.2 18.9 %all_gather.6 = f32[256,130]{1,0:T(8,128)S(1)} all-gather(f32[16,130]{1,0:T(8,128)S(1)} %pad_maximum_fusion.5), channel_id=1, replica_groups=mesh['bunch'=16,'mp'=16] {'bunch'}, dimensions={0}, use_global_device_ids=true | all-gather | bytes 141440 | tf_op jit(solution)/shard_map/all_gather | solution.py:27
  96.1 57.1 %while.47 = (s32[]{:T(128)}, f32[16,3,4096]{2,0,1:T(8,128)S(1)}, f32[16,3,256]{2,0,1:T(8,128)S(1)}, s32[16,4096]{1,0:T(8,128)}, s32[]{:T(128)}, /*index=5*/s32[]{:T(128)}) while((s32[]{:T(128)}, f32[16,3,4096]{2,0,1:T(8,128)S(1)}, f32[16,3,256]{2,0,1:T(8,128)S(1)}, s32[16,4096]{1,0:T(8,128)}, s32[]{:T(128)}, ...), condition=%wide.region_4.5_spmd.clone, body=%wide.region_3.4_spmd.clone.sunk | while | flops 38797312 | bytes 304217 | solution.py:88
  118.5 2.1 convolution_bitcast_fusion.6
  122.0 2.1 convolution_bitcast_fusion.6
  125.6 2.1 convolution_bitcast_fusion.6
  129.2 2.1 convolution_bitcast_fusion.6
  132.8 2.1 convolution_bitcast_fusion.6
  136.3 2.1 convolution_bitcast_fusion.6
  139.9 2.1 convolution_bitcast_fusion.6
  143.5 2.1 convolution_bitcast_fusion.6
  147.0 2.1 convolution_bitcast_fusion.6
  153.2 2.2 fusion.64
  155.5 3.0 multiply_add_fusion.5
  158.6 40.9 %while.48 = (s32[]{:T(128)}, f32[16,3,256]{2,0,1:T(8,128)S(1)}, f32[16,4096]{1,0:T(8,128)}, f32[16,4096]{1,0:T(8,128)}, s32[16,4096]{1,0:T(8,128)S(1)}, /*index=5*/s32[]{:T(128)}, f32[]{:T(128)}, f32[]{:T(128)}, s32[]{:T(128)}) while((s32[]{:T(128)}, f32[16,3,256]{2,0,1:T(8,128)S(1)}, f32[16,4096]{1,0:T(8,128)}, ...), condition=%wide.region_7.8_spmd.clone, body=%wide.region_6.7_spmd.clone.sunk | while | flops 38821888 | bytes 162961 | solution.py:74
  200.5 12.4 %all-to-all-start.1 = ((f32[16,16,3,256]{3,1,2,0:T(8,128)}), f32[16,16,3,256]{3,1,2,0:T(8,128)}, u32[]{:S(2)}, u32[]{:S(2)}) async-start(f32[16,16,3,256]{3,1,2,0:T(8,128)} %broadcast_in_dim.41), calls=%async_computation.1 | async-start | bytes 1572864 | tf_op jit(solution)/shard_map/all_to_all | solution.py:15
  214.1 21.5 %all-to-all-done.1 = f32[16,16,3,256]{3,1,2,0:T(8,128)} async-done(((f32[16,16,3,256]{3,1,2,0:T(8,128)}), f32[16,16,3,256]{3,1,2,0:T(8,128)}, u32[]{:S(2)}, u32[]{:S(2)}) %all-to-all-start.1) | async-done | bytes 786464 | tf_op jit(solution)/shard_map/all_to_all | solution.py:15
  237.0 17.8 %all_gather.7 = f32[256,130]{1,0:T(8,128)S(1)} all-gather(f32[16,130]{1,0:T(8,128)S(1)} %pad_maximum_fusion.6), channel_id=1, replica_groups=mesh['bunch'=16,'mp'=16] {'bunch'}, dimensions={0}, use_global_device_ids=true | all-gather | bytes 141440 | tf_op jit(solution)/shard_map/all_gather | solution.py:27
  257.5 57.1 %while.49 = (s32[]{:T(128)}, f32[16,3,4096]{2,0,1:T(8,128)S(1)}, f32[16,3,256]{2,0,1:T(8,128)S(1)}, s32[16,4096]{1,0:T(8,128)}, s32[]{:T(128)}, /*index=5*/s32[]{:T(128)}) while((s32[]{:T(128)}, f32[16,3,4096]{2,0,1:T(8,128)S(1)}, f32[16,3,256]{2,0,1:T(8,128)S(1)}, s32[16,4096]{1,0:T(8,128)}, s32[]{:T(128)}, ...), condition=%wide.region_10.11_spmd.clone, body=%wide.region_9.10_spmd.clone.sunk | while | flops 38797312 | bytes 304217 | solution.py:88
  258.5 2.1 convolution_bitcast_fusion.7
  315.3 3.2 %multiply_add_fusion.3 = (f32[1,16,4096]{2,1,0:T(8,128)S(1)}, f32[1,16,4096]{2,1,0:T(8,128)S(1)}, f32[1,16,4096]{2,1,0:T(8,128)S(1)}, f32[1,16,4096]{2,1,0:T(8,128)S(1)}, f32[1,16,4096]{2,1,0:T(8,128)S(1)}) fusion(f32[16]{0:T(128)S(1)} %get-tuple-element.282, f32[16]{0:T(128)S(1)} %get-tuple-element.280, f32[16,3,4096]{2,0,1:T(8,128)S(1)} %get-tuple-element.123, ...), kind=kLoop, calls=%fused_computation.77 | loop fusion | flops 2359296 | bytes 3408128 | tf_op jit(solution)/shard_map/add | solution.py:95
  318.5 2.2 multiply_add_fusion.1
  (487 shorter events, 204.9 us)
Async XLA Ops:
  0.6 95.0 %copy-start = (f32[256,256]{1,0:T(8,128)S(1)}, f32[256,256]{1,0:T(8,128)}, u32[]{:S(2)}) copy-start(f32[256,256]{1,0:T(8,128)} %param.19) | copy-start | bytes 786436
  0.6 1.2 copy-start.8
  27.5 1.0 copy-start.7
  27.5 11.0 %copy-start.10 = (f32[2,64,16]{1,2,0:T(8,128)S(1)}, f32[2,64,16]{1,2,0:T(8,128)}, u32[]{:S(2)}) copy-start(f32[2,64,16]{1,2,0:T(8,128)} %param.17) | copy-start | bytes 24580
  27.5 11.1 %copy-start.9 = (f32[16640]{0:T(1024)S(1)}, f32[16640]{0:T(1024)}, u32[]{:S(2)}) copy-start(f32[16640]{0:T(1024)} %param.18) | copy-start | bytes 199684
  28.5 46.4 %all-to-all-start = ((f32[16,16,3,256]{3,1,2,0:T(8,128)}), f32[16,16,3,256]{3,1,2,0:T(8,128)S(1)}, u32[]{:S(2)}, u32[]{:S(2)}) async-start(f32[16,16,3,256]{3,1,2,0:T(8,128)} %broadcast_in_dim.39), calls=%async_computation | async-start | bytes 1572864 | tf_op jit(solution)/shard_map/all_to_all | solution.py:15
  75.0 20.4 %copy-start.4 = (f32[256,256]{1,0:T(8,128)S(1)}, f32[256,256]{1,0:T(8,128)}, u32[]{:S(2)}) copy-start(f32[256,256]{1,0:T(8,128)} %param.20) | copy-start | bytes 786436
  153.2 2.3 copy-start.11
  153.2 2.3 copy-start.1
  199.5 1.0 copy-start.6
  200.5 35.2 %all-to-all-start.1 = ((f32[16,16,3,256]{3,1,2,0:T(8,128)}), f32[16,16,3,256]{3,1,2,0:T(8,128)}, u32[]{:S(2)}, u32[]{:S(2)}) async-start(f32[16,16,3,256]{3,1,2,0:T(8,128)} %broadcast_in_dim.41), calls=%async_computation.1 | async-start | bytes 1572864 | tf_op jit(solution)/shard_map/all_to_all | solution.py:15
  214.1 40.7 %copy-start.5 = (f32[256,256]{1,0:T(8,128)S(1)}, f32[256,256]{1,0:T(8,128)}, u32[]{:S(2)}) copy-start(f32[256,256]{1,0:T(8,128)} %param.20) | copy-start | bytes 786436
  257.5 57.8 %copy-start.2 = (f32[1,16,4096]{2,1,0:T(8,128)S(1)}, f32[1,16,4096]{2,1,0:T(8,128)}, u32[]{:S(2)}) copy-start(f32[1,16,4096]{2,1,0:T(8,128)} %get-tuple-element.256) | copy-start | bytes 786436
  257.5 57.8 %copy-start.3 = (f32[1,16,4096]{2,1,0:T(8,128)S(1)}, f32[1,16,4096]{2,1,0:T(8,128)}, u32[]{:S(2)}) copy-start(f32[1,16,4096]{2,1,0:T(8,128)} %get-tuple-element.257) | copy-start | bytes 786436
where the time goes:
time: 324 us; the launch traced here: 322 us
  matrix products  119 us (37%)
  local copies, waits for them, and re-layouts  106 us (33%)
  blocking collectives  36.6 us (11%)
  starting transfers between devices  22.4 us (7%)
  waiting for transfers between devices  21.5 us (7%)
  other arithmetic  12.1 us (4%)
  loops' own time  3.33 us (1%)
    dot_general x32, matrix products, lookup(): lax.dot_general(kick_rows, onehot, (((1,), (1,)), ((), ())), precision=hi...  68 us
    dynamic_slice x96, local copies, waits for them, and re-layouts, body(): moments = lax.map(moments_of, (slice_row, coords[0], coords[2]))  46.7 us
    dot_general x32, matrix products, moments_of(): jnp.dot(stacked, onehot, precision=highest, preferred_element_type=jnp.fl...  46.3 us
    all_gather x2, blocking collectives, gather_turned(): whole = lax.all_gather(both, axis, axis=0, tiled=True)  36.6 us
    gather x64, local copies, waits for them, and re-layouts  35.7 us
    all_to_all x2, starting transfers between devices, sent_to_all(): return lax.all_to_all(copies, axis, split_axis=0, concat_axis=0, tiled=True)  22.4 us
    all_to_all x2, waiting for transfers between devices, sent_to_all(): return lax.all_to_all(copies, axis, split_axis=0, concat_axis=0, tiled=True)  21.5 us
    dynamic_update_slice x64, local copies, waits for them, and re-layouts, body(): picked = lax.map(lookup, (slice_row, kick_table))  14.9 us
  transfers between devices with their start and end apart: 2, of which 1 were waited for; matrix products, arithmetic and copies ran while one was open for 12% of the time, Pallas kernels for 0%

commit v1 on v0

v1 whole, which is shorter than its diff:
```python
import functools

import jax
import jax.numpy as jnp
from jax import lax
from jax.experimental import pallas as pl
from jax.experimental.pallas import tpu as pltpu
from jax.sharding import PartitionSpec as P

SLICES = 256
TURNS = 2
DETUNE = 0.02
LANES = 128
COARSE, FINE = 8, 32
CHUNK = 512
GROUP = 8

F32, BF16, I32 = jnp.float32, jnp.bfloat16, jnp.int32
NT = (((1,), (1,)), ((), ()))
HIGHEST = lax.Precision.HIGHEST


def iota(shape, axis):
    return lax.broadcasted_iota(I32, shape, axis)


def gather_lanes(row, index):
    return jnp.take_along_axis(row, index, axis=1, mode="promise_in_bounds")


def two_pieces(v):
    high = v.astype(BF16).astype(F32)
    return high, v - high


def sin_cos(theta):
    n = jnp.round(theta * 0.6366197723675814)
    r = theta - n * 1.5703125
    r = r - n * 4.837512969970703e-4
    r = r - n * 7.549789948768648e-8
    r = jnp.clip(r, -0.8, 0.8)
    q = n.astype(I32)
    z = r * r
    s = r + r * z * (-1.6666654611e-1 + z * (8.3321608736e-3 + z * -1.9515295891e-4))
    c = 1.0 - 0.5 * z + z * z * (
        4.166664568298827e-2 + z * (-1.388731625493765e-3 + z * 2.443315711809948e-5)
    )
    odd = (q & 1) == 1
    sin, cos = jnp.where(odd, c, s), jnp.where(odd, s, c)
    sin = jnp.where((q & 2) == 2, -sin, sin)
    cos = jnp.where(((q + 1) & 2) == 2, -cos, cos)
    return sin, cos


def kernel(
    rings,
    phase_ref,
    advance_ref,
    hist_ref,
    wake_ref,
    dipole_ref,
    quad_ref,
    ids_ref,
    out_ref,
    cent_ref,
    msg,
    landed,
    far_src,
    far_all,
    tab_src,
    tab_all,
    spread,
    ext,
    toep0,
    rot,
    msg_send,
    msg_recv,
    far_send,
    far_recv,
    tab_send,
    tab_recv,
):
    n_bunch, n_mp = rings
    me_b, me_m = lax.axis_index("bunch"), lax.axis_index("mp")
    bunches, parts = phase_ref.shape[1], phase_ref.shape[2]
    scale = 1.0 / (parts * n_mp)

    barrier = pltpu.get_barrier_semaphore()

    def greet(k, _):
        pl.semaphore_signal(barrier, inc=1, device_id={"mp": lax.rem(me_m + k, n_mp)})
        pl.semaphore_signal(barrier, inc=1, device_id={"bunch": lax.rem(me_b + k, n_bunch)})
        return 0

    lax.fori_loop(1, 16, greet, 0)

    def msg_copy(turn, b):
        return pltpu.make_async_remote_copy(
            src_ref=msg.at[turn, b],
            dst_ref=landed.at[turn, me_m],
            send_sem=msg_send.at[turn, b],
            recv_sem=msg_recv.at[turn, me_m],
            device_id={"mp": b},
        )

    def msg_arrival(turn, sender):
        return pltpu.make_async_remote_copy(
            src_ref=msg.at[turn, sender],
            dst_ref=landed.at[turn, sender],
            send_sem=msg_send.at[turn, sender],
            recv_sem=msg_recv.at[turn, sender],
            device_id={"mp": sender},
        )

    def far_copy(kind, peer):
        return pltpu.make_async_remote_copy(
            src_ref=far_src.at[kind],
            dst_ref=far_all.at[kind, me_b],
            send_sem=far_send.at[kind, peer],
            recv_sem=far_recv.at[kind, me_b],
            device_id={"bunch": peer},
        )

    def far_arrival(kind, peer):
        return pltpu.make_async_remote_copy(
            src_ref=far_src.at[kind],
            dst_ref=far_all.at[kind, peer],
            send_sem=far_send.at[kind, peer],
            recv_sem=far_recv.at[kind, peer],
            device_id={"bunch": peer},
        )

    def tab_copy(turn, peer):
        return pltpu.make_async_remote_copy(
            src_ref=tab_src.at[turn],
            dst_ref=tab_all.at[turn, me_m],
            send_sem=tab_send.at[turn, peer],
            recv_sem=tab_recv.at[turn, me_m],
            device_id={"mp": peer},
        )

    def tab_arrival(turn, peer):
        return pltpu.make_async_remote_copy(
            src_ref=tab_src.at[turn],
            dst_ref=tab_all.at[turn, peer],
            send_sem=tab_send.at[turn, peer],
            recv_sem=tab_recv.at[turn, peer],
            device_id={"mp": peer},
        )

    def others(me, n, act):
        def step(k, _):
            act(lax.rem(me + k, n))
            return 0

        lax.fori_loop(1, n, step, 0)

    row8, lane8 = iota((8, LANES), 0), iota((8, LANES), 1)
    place = lax.rem(me_b, 8) * bunches

    share = hist_ref.shape[1] // n_mp
    own = jnp.concatenate(
        [hist_ref[0, pl.ds(me_m * share, share), :], hist_ref[1, pl.ds(me_m * share, share), :]], axis=0
    )
    own = jnp.concatenate([own, jnp.zeros((8, LANES - bunches), F32)], axis=1)
    own = pltpu.roll(own, place, 1)
    far_src[2] = own
    far_all[2, me_b] = own
    spread[...] = jnp.zeros_like(spread)

    def send_sums(turn, sums_x, sums_y):
        spread[0, pl.ds(place, bunches), :] = sums_x * scale
        spread[1, pl.ds(place, bunches), :] = sums_y * scale
        ones = jnp.ones((8, LANES), F32)
        row_x = lax.dot_general(ones, spread[0], NT, precision=HIGHEST, preferred_element_type=F32)
        row_y = lax.dot_general(ones, spread[1], NT, precision=HIGHEST, preferred_element_type=F32)
        tile = jnp.where(row8 == 0, row_x, row_y)
        far_src[turn] = tile
        far_all[turn, me_b] = tile

    def lane_sums(p):
        def step(c, acc):
            return acc + phase_ref[p, :, pl.ds(pl.multiple_of(c * LANES, LANES), LANES)]

        return lax.fori_loop(0, parts // LANES, step, jnp.zeros((bunches, LANES), F32), unroll=8)

    send_sums(0, lane_sums(0), lane_sums(2))

    diag = iota((bunches, LANES), 0) == iota((bunches, LANES), 1)
    for p in range(2):
        wide = jnp.concatenate([advance_ref[p : p + 1, :], jnp.zeros((1, LANES - bunches), F32)], axis=1)
        column = jnp.sum(jnp.where(diag, jnp.broadcast_to(wide, (bunches, LANES)), 0.0), axis=1, keepdims=True)
        sin, cos = sin_cos(jnp.broadcast_to(column, (bunches, LANES)))
        rot[2 * p] = cos
        rot[2 * p + 1] = sin

    pl.semaphore_wait(barrier, n_mp + n_bunch - 2)
    others(me_b, n_bunch, lambda peer: far_copy(2, peer).start())
    others(me_b, n_bunch, lambda peer: far_copy(0, peer).start())

    iota_c = iota((COARSE, CHUNK), 0)
    iota_f = iota((FINE, CHUNK), 0)
    own_lanes = lax.shift_right_logical(lane8, 5) == (row8 & 3)

    def bin_bunch(turn, source, b):
        acc = None
        for c in range(parts // CHUNK):
            at = pl.ds(c * CHUNK, CHUNK)
            ids = ids_ref[turn, pl.ds(b, 1), at]
            x = source[0, pl.ds(b, 1), at]
            y = source[2, pl.ds(b, 1), at]
            coarse = iota_c == lax.shift_right_logical(ids, 5)
            fine = jnp.where(iota_f == (ids & (FINE - 1)), 1.0, 0.0).astype(BF16)
            rows = [jnp.where(coarse, 1.0, 0.0)]
            for v in (*two_pieces(x), *two_pieces(y)):
                rows.append(jnp.where(coarse, jnp.broadcast_to(v, (COARSE, CHUNK)), 0.0))
            weighted = jnp.concatenate(rows, axis=0).astype(BF16)
            part = lax.dot_general(weighted, fine, NT, preferred_element_type=F32)
            acc = part if acc is None else acc + part
        tiles = []
        for v in (acc[8:16] + acc[16:24], acc[24:32] + acc[32:40], acc[0:8]):
            v = jnp.where(own_lanes, jnp.concatenate([v] * 4, axis=1), 0.0)
            v = v + pltpu.roll(v, 1, 0)
            tiles.append(v + pltpu.roll(v, 2, 0))
        last = row8 & 3
        tile = jnp.where(
            last == 3,
            tiles[0],
            jnp.where(last == 0, pltpu.roll(tiles[1], 1, 0), pltpu.roll(tiles[2], 2, 0)),
        )
        msg[turn, b] = tile * scale

    def finish(turn, b):
        row_x = jnp.broadcast_to(ext[turn, 0, pl.ds(b, 1), :], (8, LANES))
        row_y = jnp.broadcast_to(ext[turn, 1, pl.ds(b, 1), :], (8, LANES))
        tile = jnp.where(row8 == 2, row_x, jnp.where(row8 == 6, row_y, msg[turn, b]))
        msg[turn, b] = tile

    def toeplitz_rows(r, half, sub):
        d = place_all + sub * 8 + row8 - (LANES * half + lane8) - 1
        c = d & (SLICES - 1)
        index = c & (LANES - 1)
        low = jnp.broadcast_to(wake_ref[pl.ds(2 * r, 1), :], (8, LANES))
        high = jnp.broadcast_to(wake_ref[pl.ds(2 * r + 1, 1), :], (8, LANES))
        return jnp.where(c >= LANES, gather_lanes(high, index), gather_lanes(low, index)), d >= 0

    place_all = me_b * bunches

    def collected(kind):
        halves = []
        for half in range(2):
            total = far_all[kind, 8 * half]
            for k in range(1, 8):
                total = total + far_all[kind, 8 * half + k]
            halves.append(total)
        return halves

    def row_of(tile, k):
        return jnp.broadcast_to(tile[k : k + 1, :], (8, LANES))

    top = hist_ref.shape[1]

    def far_first():
        others(me_b, n_bunch, lambda peer: far_arrival(2, peer).wait_recv())
        others(me_b, n_bunch, lambda peer: far_arrival(0, peer).wait_recv())
        hist, cent = collected(2), collected(0)
        kept = jnp.where(me_m == n_mp - 1, 0.0, 1.0)
        for sub in range(2):
            at = pl.ds(8 * sub, 8)
            sums = [[jnp.zeros((8, LANES), F32) for _ in range(2)] for _ in range(2)]
            for half in range(2):
                g0, upper = toeplitz_rows(0, half, sub)
                g1, _ = toeplitz_rows(1, half, sub)
                u0 = jnp.where(upper, g0, 0.0)
                u1 = jnp.where(upper, g1, g0)
                toep0[half, at, :] = u0
                for p in range(2):
                    c = row_of(cent[half], p)
                    sums[0][p] = sums[0][p] + u0 * c
                    sums[1][p] = sums[1][p] + u1 * c
                first = me_m * share
                g = [
                    toeplitz_rows(jnp.minimum(first + k, top), half, sub)[0] for k in range(share + 2)
                ]
                for k in range(share):
                    near = jnp.where(upper, g[k + 1], g[k])
                    later = jnp.where(upper, g[k + 2], g[k + 1])
                    if k == share - 1:
                        later = later * kept
                    for p in range(2):
                        h = row_of(hist[half], p * share + k)
                        sums[0][p] = sums[0][p] + near * h
                        sums[1][p] = sums[1][p] + later * h
            for turn in range(2):
                for p in range(2):
                    ext[turn, p, at, :] = sums[turn][p]

    def far_second():
        others(me_b, n_bunch, lambda peer: far_arrival(1, peer).wait_recv())
        cent = collected(1)
        for sub in range(2):
            at = pl.ds(8 * sub, 8)
            for p in range(2):
                total = ext[1, p, at, :]
                for half in range(2):
                    total = total + toep0[half, at, :] * row_of(cent[half], p)
                ext[1, p, at, :] = total

    early = bunches // 2

    def one_turn(turn, source):
        def bin_early(k, _):
            bin_bunch(turn, source, lax.rem(me_m + 1 + k, n_mp))
            return 0

        lax.fori_loop(0, early, bin_early, 0)
        (far_first if turn == 0 else far_second)()

        def send_early(k, _):
            b = lax.rem(me_m + 1 + k, n_mp)
            finish(turn, b)
            msg_copy(turn, b).start()
            return 0

        lax.fori_loop(0, early, send_early, 0)

        def bin_late(k, _):
            b = lax.rem(me_m + 1 + k, n_mp)
            bin_bunch(turn, source, b)
            finish(turn, b)
            msg_copy(turn, b).start()
            return 0

        lax.fori_loop(early, bunches - 1, bin_late, 0)
        bin_bunch(turn, source, me_m)
        finish(turn, me_m)
        landed[turn, me_m] = msg[turn, me_m]

        others(me_m, n_mp, lambda peer: msg_arrival(turn, peer).wait_recv())
        total = landed[turn, 0]
        for k in range(1, 16):
            total = total + landed[turn, k]
        wide = jnp.concatenate([total, pltpu.roll(total, 4, 0)], axis=1)
        dip = lax.dot_general(wide, dipole_ref[...], NT, precision=HIGHEST, preferred_element_type=F32)
        quad = lax.dot_general(wide, quad_ref[...], NT, precision=HIGHEST, preferred_element_type=F32)
        moved = jnp.sum(wide, axis=1, keepdims=True)
        ext_sum = jnp.sum(total, axis=1, keepdims=True)
        low, high = dip[:, :LANES], dip[:, LANES:]
        far_x = jnp.broadcast_to(ext_sum[2:3], (1, LANES))
        far_y = jnp.broadcast_to(ext_sum[6:7], (1, LANES))
        tab_src[turn] = jnp.concatenate(
            [
                low[3:4] + far_x,
                high[3:4] + far_x,
                low[4:5] + far_y,
                high[4:5] + far_y,
                quad[5:6, :LANES],
                quad[5:6, LANES:],
                jnp.broadcast_to(moved[3:4], (1, LANES)),
                jnp.broadcast_to(moved[4:5], (1, LANES)),
            ],
            axis=0,
        )
        others(me_m, n_mp, lambda peer: tab_copy(turn, peer).start())
        tab_all[turn, me_m] = tab_src[turn]
        others(me_m, n_mp, lambda peer: tab_arrival(turn, peer).wait_recv())

        table = tab_all.at[turn]

        def column(k, first, count):
            return jnp.concatenate([table[first + n, k : k + 1, :] for n in range(count)], axis=0)

        for p in range(2):
            spot = jnp.where(diag, column(6 + p, 0, bunches), 0.0)
            cent_ref[p, turn : turn + 1, :] = jnp.sum(spot, axis=0, keepdims=True)[:, :bunches]

        sums = []
        for g in range(bunches // GROUP):
            at = pl.ds(g * GROUP, GROUP)
            rows = [column(k, g * GROUP, GROUP) for k in range(6)]
            cos_x, sin_x, cos_y, sin_y = (rot[k, at, :] for k in range(4))

            def kick(c, acc):
                lanes = pl.ds(pl.multiple_of(c * LANES, LANES), LANES)
                ids = ids_ref[turn, at, lanes]
                x, mx, y, my = (source[k, at, lanes] for k in range(4))
                index, upper = ids & (LANES - 1), ids >= LANES
                kx, ky, kq = (
                    jnp.where(upper, gather_lanes(rows[2 * k + 1], index), gather_lanes(rows[2 * k], index))
                    for k in range(3)
                )
                mx = mx + (kx + kq * x)
                my = my + (ky - kq * y)
                action = x * x + mx * mx + y * y + my * my
                sin, cos = sin_cos(DETUNE * action)
                x, mx = cos * x + sin * mx, cos * mx - sin * x
                y, my = cos * y + sin * my, cos * my - sin * y
                x, mx = cos_x * x + sin_x * mx, cos_x * mx - sin_x * x
                y, my = cos_y * y + sin_y * my, cos_y * my - sin_y * y
                out_ref[0, at, lanes] = x
                out_ref[1, at, lanes] = mx
                out_ref[2, at, lanes] = y
                out_ref[3, at, lanes] = my
                return acc[0] + x, acc[1] + y

            zero = jnp.zeros((GROUP, LANES), F32)
            sums.append(lax.fori_loop(0, parts // LANES, kick, (zero, zero), unroll=4))
        if turn == 0:
            send_sums(1, *(jnp.concatenate([s[p] for s in sums], axis=0) for p in range(2)))
            others(me_b, n_bunch, lambda peer: far_copy(1, peer).start())

    one_turn(0, phase_ref)
    one_turn(1, out_ref)

    for turn in range(TURNS):
        others(me_m, n_mp, lambda peer: msg_copy(turn, peer).wait_send())
        others(me_m, n_mp, lambda peer: tab_copy(turn, peer).wait_send())
    for kind in range(3):
        others(me_b, n_bunch, lambda peer: far_copy(kind, peer).wait_send())


def body(phase_space, phase_advance, centroid_history, lr_wake, sr_dipole, sr_quad, slice_ids):
    n_bunch, n_mp = lax.axis_size("bunch"), lax.axis_size("mp")
    bunches = phase_space.shape[1]
    vmem = pl.BlockSpec(memory_space=pltpu.VMEM)
    dma = pltpu.SemaphoreType.DMA
    return tuple(
        pl.pallas_call(
            functools.partial(kernel, (n_bunch, n_mp)),
            out_shape=(
                jax.ShapeDtypeStruct(phase_space.shape, F32),
                jax.ShapeDtypeStruct((2, TURNS, bunches), F32),
            ),
            in_specs=[vmem] * 7,
            out_specs=(vmem, vmem),
            scratch_shapes=[
                pltpu.VMEM((TURNS, bunches, 8, LANES), F32),
                pltpu.VMEM((TURNS, n_mp, 8, LANES), F32),
                pltpu.VMEM((3, 8, LANES), F32),
                pltpu.VMEM((3, n_bunch, 8, LANES), F32),
                pltpu.VMEM((TURNS, 8, LANES), F32),
                pltpu.VMEM((TURNS, n_mp, 8, LANES), F32),
                pltpu.VMEM((2, LANES, LANES), F32),
                pltpu.VMEM((TURNS, 2, bunches, LANES), F32),
                pltpu.VMEM((2, bunches, LANES), F32),
                pltpu.VMEM((4, bunches, LANES), F32),
                dma((TURNS, n_mp)),
                dma((TURNS, n_mp)),
                dma((3, n_bunch)),
                dma((3, n_bunch)),
                dma((TURNS, n_mp)),
                dma((TURNS, n_mp)),
            ],
            compiler_params=pltpu.CompilerParams(
                collective_id=0, has_side_effects=True, vmem_limit_bytes=32 << 20
            ),
            cost_estimate=pl.CostEstimate(
                flops=4 * 65536 * 256, bytes_accessed=3 << 20, transcendentals=0
            ),
        )(
            phase_space,
            phase_advance,
            centroid_history,
            lr_wake.reshape(-1, LANES),
            sr_dipole,
            sr_quad,
            slice_ids,
        )
    )


def solution(mesh):
    placed = (
        P(None, "bunch", "mp"),
        P(None, "bunch"),
        P(None, None, "bunch"),
        P(),
        P(),
        P(),
        P(None, "bunch", "mp"),
    )
    return jax.shard_map(
        body,
        mesh=mesh,
        in_specs=placed,
        out_specs=(P(None, "bunch", "mp"), P(None, None, "bunch")),
        check_vma=False,
    )
```

time: 324 us -> 58.7 us (0.18)
  matrix products: 119 us -> 0 us
  local copies, waits for them, and re-layouts: 106 us -> 6.58 us
  Pallas kernels: 0 us -> 51.2 us
  blocking collectives: 36.6 us -> 0 us
  starting transfers between devices: 22.4 us -> 0 us
  waiting for transfers between devices: 21.5 us -> 0 us
  other arithmetic: 12.1 us -> 0 us
  loops' own time: 3.33 us -> 0 us
    dot_general x70 -> x0, matrix products: 119 us -> none  [the longest x32 68 us: lookup(): lax.dot_general(kick_rows, onehot, (((1,), (1,)), ((), ())), precision=hi...]
    pallas_call x0 -> x1, Pallas kernels: none -> 51.2 us  [body(): pl.pallas_call(functools.partial(kernel, (n_bunch, n_mp)), out_shape=(jax...]
    dynamic_slice x128 -> x0, local copies, waits for them, and re-layouts: 47.1 us -> none  [the longest x96 46.7 us: body(): moments = lax.map(moments_of, (slice_row, coords[0], coords[2]))]
    all_gather x2 -> x0, blocking collectives: 36.6 us -> none  [gather_turned(): whole = lax.all_gather(both, axis, axis=0, tiled=True)]
    gather x64 -> x0, local copies, waits for them, and re-layouts: 35.7 us -> none
    all_to_all x2 -> x0, starting transfers between devices: 22.4 us -> none  [sent_to_all(): return lax.all_to_all(copies, axis, split_axis=0, concat_axis=0, tiled=True)]
    all_to_all x2 -> x0, waiting for transfers between devices: 21.5 us -> none  [sent_to_all(): return lax.all_to_all(copies, axis, split_axis=0, concat_axis=0, tiled=True)]
    dynamic_update_slice x128 -> x0, local copies, waits for them, and re-layouts: 16.3 us -> none  [the longest x64 14.9 us: body(): picked = lax.map(lookup, (slice_row, kick_table))]
  transfers between devices with their start and end apart: 2 -> 0, of which waited for: 1 -> 0; matrix products, arithmetic and copies ran while one was open for 12% -> 0% of each run, Pallas kernels for 0% -> 0%
where the time goes in v1:
time: 58.7 us; the launch traced here: 58.4 us
  Pallas kernels  51.2 us (87%)
  local copies, waits for them, and re-layouts  6.58 us (11%)
  between operations  0.66 us (1%)
    pallas_call x1, Pallas kernels, body(): pl.pallas_call(functools.partial(kernel, (n_bunch, n_mp)), out_shape=(jax...  51.2 us
    unnamed x15, local copies, waits for them, and re-layouts  6.58 us

profile of v1, /device:TPU:1, one launch (start us, length us, event | category | flops | bytes accessed | tf_op | source)
XLA Modules:
  0.0 58.4 jit_solution(7250995824266567896)
XLA Ops:
  0.6 0.0 copy-start.4
  0.6 0.0 copy-start.5
  0.7 0.8 %copy.9.hist_ref = f32[2,64,16]{2,1,0:T(8,128)S(1)} copy(f32[2,64,16]{1,2,0:T(8,128)} %param.9) | data formatting | bytes 16384 | tf_op args[2]
  1.5 0.0 copy-done.4
  1.5 0.0 copy-done.5
  1.5 0.0 copy-start
  1.5 1.2 %copy-done = f32[4,16,4096]{2,1,0:T(8,128)S(1)} copy-done((f32[4,16,4096]{2,1,0:T(8,128)S(1)}, f32[4,16,4096]{2,1,0:T(8,128)}, u32[]{:S(2)}) %copy-start) | copy-done | bytes 1048600
  2.7 0.0 copy-start.1
  2.7 1.0 %copy-done.1 = s32[2,16,4096]{2,1,0:T(8,128)S(1)} copy-done((s32[2,16,4096]{2,1,0:T(8,128)S(1)}, s32[2,16,4096]{2,1,0:T(8,128)}, u32[]{:S(2)}) %copy-start.1) | copy-done | bytes 524312
  3.8 0.0 copy-start.2
  3.8 0.9 %copy-done.2 = f32[256,256]{1,0:T(8,128)S(1)} copy-done((f32[256,256]{1,0:T(8,128)S(1)}, f32[256,256]{1,0:T(8,128)}, u32[]{:S(2)}) %copy-start.2) | copy-done | bytes 262168
  4.7 0.0 copy-start.3
  4.7 0.9 %copy-done.3 = f32[256,256]{1,0:T(8,128)S(1)} copy-done((f32[256,256]{1,0:T(8,128)S(1)}, f32[256,256]{1,0:T(8,128)}, u32[]{:S(2)}) %copy-start.3) | copy-done | bytes 262168
  5.7 51.2 %shard_map.86 = (f32[4,16,4096]{2,1,0:T(8,128)S(1)}, f32[2,2,16]{2,1,0:T(2,128)S(1)}) custom-call(f32[4,16,4096]{2,1,0:T(8,128)S(1)} %copy-done, f32[2,16]{1,0:T(2,128)S(1)} %copy-done.5, f32[2,64,16]{2,1,0:T(8,128)S(1)} %copy.9.hist_ref, f32[130,128]{1,0:T(8,128)S(1)} %bitcast.1, f32[256,256]{1,0:T(8,128)S(1)} %copy-done.2, f32[256,256]{1,0:T(8,128)S(1)} %copy-done.3, ...), custom_call_target="tpu_custom_call" | custom-call | flops 67108864 | bytes 3145728 | tf_op jit(solution)/shard_map/pallas_call | solution.py:428
  56.8 1.0 %copy.12 = f32[4,16,4096]{2,1,0:T(8,128)} copy(f32[4,16,4096]{2,1,0:T(8,128)S(1)} %get-tuple-element.4) | data formatting | bytes 2097152
  57.8 0.6 copy.13
Async XLA Ops:
  0.6 0.9 %copy-start.4 = (f32[16640]{0:T(1024)S(1)}, f32[16640]{0:T(1024)}, u32[]{:S(2)}) copy-start(f32[16640]{0:T(1024)} %param.10) | copy-start | bytes 199684
  0.6 0.9 %copy-start.5 = (f32[2,16]{1,0:T(2,128)S(1)}, f32[2,16]{1,0:T(2,128)}, u32[]{:S(2)}) copy-start(f32[2,16]{1,0:T(2,128)} %advance_ref.1) | copy-start | bytes 388
  1.5 1.2 %copy-start = (f32[4,16,4096]{2,1,0:T(8,128)S(1)}, f32[4,16,4096]{2,1,0:T(8,128)}, u32[]{:S(2)}) copy-start(f32[4,16,4096]{2,1,0:T(8,128)} %phase_ref.1) | copy-start | bytes 3145732
  2.7 1.0 %copy-start.1 = (s32[2,16,4096]{2,1,0:T(8,128)S(1)}, s32[2,16,4096]{2,1,0:T(8,128)}, u32[]{:S(2)}) copy-start(s32[2,16,4096]{2,1,0:T(8,128)} %ids_ref.1) | copy-start | bytes 1572868
  3.8 0.9 %copy-start.2 = (f32[256,256]{1,0:T(8,128)S(1)}, f32[256,256]{1,0:T(8,128)}, u32[]{:S(2)}) copy-start(f32[256,256]{1,0:T(8,128)} %dipole_ref.1) | copy-start | bytes 786436
  4.7 0.9 %copy-start.3 = (f32[256,256]{1,0:T(8,128)S(1)}, f32[256,256]{1,0:T(8,128)}, u32[]{:S(2)}) copy-start(f32[256,256]{1,0:T(8,128)} %quad_ref.1) | copy-start | bytes 786436

commit v2 on v1

v2 whole, which is shorter than its diff:
```python
import functools

import jax
import jax.numpy as jnp
from jax import lax
from jax.experimental import pallas as pl
from jax.experimental.pallas import tpu as pltpu
from jax.sharding import PartitionSpec as P

SLICES = 256
TURNS = 2
DETUNE = 0.02
LANES = 128
COARSE, FINE = 8, 32
CHUNK = 512
GROUP = 8
AT_ONCE = 4
WIDTH = 512
SPANS = 2

F32, BF16, I32 = jnp.float32, jnp.bfloat16, jnp.int32
NT = (((1,), (1,)), ((), ()))
HIGHEST = lax.Precision.HIGHEST


def iota(shape, axis):
    return lax.broadcasted_iota(I32, shape, axis)


def gather_lanes(row, index):
    return jnp.take_along_axis(row, index, axis=1, mode="promise_in_bounds")


def two_pieces(v):
    high = v.astype(BF16).astype(F32)
    return high, v - high


def sin_cos(theta):
    n = jnp.round(theta * 0.6366197723675814)
    r = theta - n * 1.5703125
    r = r - n * 4.837512969970703e-4
    r = r - n * 7.549789948768648e-8
    r = jnp.clip(r, -0.8, 0.8)
    q = n.astype(I32)
    z = r * r
    s = r + r * z * (-1.6666654611e-1 + z * (8.3321608736e-3 + z * -1.9515295891e-4))
    c = 1.0 - 0.5 * z + z * z * (
        4.166664568298827e-2 + z * (-1.388731625493765e-3 + z * 2.443315711809948e-5)
    )
    odd = (q & 1) == 1
    sin, cos = jnp.where(odd, c, s), jnp.where(odd, s, c)
    sin = jnp.where((q & 2) == 2, -sin, sin)
    cos = jnp.where(((q + 1) & 2) == 2, -cos, cos)
    return sin, cos


def turned(ids, coords, rows, rot):
    width = ids.shape[1]
    index, upper = ids & (LANES - 1), ids >= LANES

    def looked_up(k):
        pieces = []
        for c in range(width // LANES):
            at = slice(c * LANES, (c + 1) * LANES)
            low, high = gather_lanes(rows[2 * k], index[:, at]), gather_lanes(rows[2 * k + 1], index[:, at])
            pieces.append(jnp.where(upper[:, at], high, low))
        return jnp.concatenate(pieces, axis=1)

    x, mx, y, my = coords
    kx, ky, kq = looked_up(0), looked_up(1), looked_up(2)
    mx = mx + (kx + kq * x)
    my = my + (ky - kq * y)
    action = x * x + mx * mx + y * y + my * my
    sin, cos = sin_cos(DETUNE * action)
    cos_x, sin_x, cos_y, sin_y = (jnp.concatenate([r] * (width // LANES), axis=1) for r in rot)
    x, mx = cos * x + sin * mx, cos * mx - sin * x
    y, my = cos * y + sin * my, cos * my - sin * y
    x, mx = cos_x * x + sin_x * mx, cos_x * mx - sin_x * x
    y, my = cos_y * y + sin_y * my, cos_y * my - sin_y * y
    return x, mx, y, my


def track_kernel(
    rings,
    phase_hbm,
    advance_hbm,
    hist_hbm,
    wake_hbm,
    dipole_hbm,
    quad_hbm,
    ids_hbm,
    mid_ref,
    next_ids,
    rows_ref,
    rot,
    cent_ref,
    phase_ref,
    first_ids,
    advance_ref,
    hist_ref,
    wake_ref,
    dipole_ref,
    quad_ref,
    msg,
    landed,
    hist_src,
    hist_all,
    sum_src,
    sum_all,
    far_src,
    far_all,
    tab_src,
    tab_all,
    spread,
    ext,
    toep0,
    load,
    msg_send,
    msg_recv,
    hist_send,
    hist_recv,
    sum_send,
    sum_recv,
    far_send,
    far_recv,
    tab_send,
    tab_recv,
):
    n_bunch, n_mp = rings
    me_b, me_m = lax.axis_index("bunch"), lax.axis_index("mp")
    bunches, parts = mid_ref.shape[1], mid_ref.shape[2]
    turns_back = hist_ref.shape[2]
    share = turns_back // n_mp
    scale = 1.0 / (parts * n_mp)

    barrier = pltpu.get_barrier_semaphore()

    def greet(k, _):
        pl.semaphore_signal(barrier, inc=1, device_id={"mp": lax.rem(me_m + k, n_mp)})
        pl.semaphore_signal(barrier, inc=1, device_id={"bunch": lax.rem(me_b + k, n_bunch)})
        return 0

    lax.fori_loop(1, 16, greet, 0)

    loads = [
        pltpu.make_async_copy(source, target, load.at[k])
        for k, (source, target) in enumerate(
            (
                (phase_hbm.at[0], phase_ref.at[0]),
                (phase_hbm.at[2], phase_ref.at[2]),
                (ids_hbm.at[0], first_ids),
                (hist_hbm, hist_ref),
                (wake_hbm, wake_ref),
                (advance_hbm, advance_ref),
                (dipole_hbm, dipole_ref),
                (quad_hbm, quad_ref),
                (phase_hbm.at[1], phase_ref.at[1]),
                (phase_hbm.at[3], phase_ref.at[3]),
                (ids_hbm.at[1], next_ids),
            )
        )
    ]
    for copy in loads:
        copy.start()

    class Exchange:
        def __init__(self, axis, me, n, source, target, send, recv):
            self.axis, self.me, self.n = axis, me, n
            self.source, self.target, self.send, self.recv = source, target, send, recv

        def copy(self, peer, slot):
            return pltpu.make_async_remote_copy(
                src_ref=self.source,
                dst_ref=self.target.at[slot],
                send_sem=self.send.at[peer],
                recv_sem=self.recv.at[slot],
                device_id={self.axis: peer},
            )

        def each(self, act):
            def step(k, _):
                act(lax.rem(self.me + lax.rem(k + self.n // 2 - 1, self.n - 1) + 1, self.n))
                return 0

            lax.fori_loop(0, self.n - 1, step, 0)

        def start(self):
            self.each(lambda peer: self.copy(peer, self.me).start())

        def arrive(self):
            self.each(lambda peer: self.copy(peer, peer).wait_recv())

        def leave(self):
            self.each(lambda peer: self.copy(peer, self.me).wait_send())

    hist_x = Exchange("bunch", me_b, n_bunch, hist_src, hist_all, hist_send, hist_recv)
    sum_x = [
        Exchange("bunch", me_b, n_bunch, sum_src.at[t], sum_all.at[t], sum_send.at[t], sum_recv.at[t])
        for t in range(TURNS)
    ]
    far_x = [
        Exchange("mp", me_m, n_mp, far_src.at[t], far_all.at[t], far_send.at[t], far_recv.at[t])
        for t in range(TURNS)
    ]
    tab_x = [
        Exchange("mp", me_m, n_mp, tab_src.at[t], tab_all.at[t], tab_send.at[t], tab_recv.at[t])
        for t in range(TURNS)
    ]

    def msg_copy(turn, b, slot):
        return pltpu.make_async_remote_copy(
            src_ref=msg.at[turn, b],
            dst_ref=landed.at[turn, slot],
            send_sem=msg_send.at[turn, b],
            recv_sem=msg_recv.at[turn, slot],
            device_id={"mp": b},
        )

    row8, lane8 = iota((8, LANES), 0), iota((8, LANES), 1)
    place = lax.rem(me_b, 8) * bunches
    ones = jnp.ones((8, LANES), F32)

    def lane_row(block):
        return lax.dot_general(ones, block, NT, precision=HIGHEST, preferred_element_type=F32)

    spread[...] = jnp.zeros_like(spread)

    def send_sums(turn, sums_x, sums_y):
        spread[0, pl.ds(place, bunches), :] = sums_x * scale
        spread[1, pl.ds(place, bunches), :] = sums_y * scale
        rows = jnp.concatenate([lane_row(spread[0])[:1], lane_row(spread[1])[:1]], axis=0)
        sum_src[turn] = rows
        sum_all[turn, me_b] = rows
        sum_x[turn].start()

    def lane_sums(p):
        def step(c, acc):
            return acc + phase_ref[p, :, pl.ds(pl.multiple_of(c * LANES, LANES), LANES)]

        return lax.fori_loop(0, parts // LANES, step, jnp.zeros((bunches, LANES), F32), unroll=8)

    loads[3].wait()
    pick = iota((8, turns_back), 1) == me_m * share + (iota((8, turns_back), 0) & (share - 1))
    halves = iota((8, turns_back), 0) < share
    own = None
    for p in range(2):
        spread[p, pl.ds(place, bunches), :turns_back] = hist_ref[p]
        chosen = jnp.where(pick & (halves if p == 0 else ~halves), 1.0, 0.0)
        part = lax.dot_general(
            chosen, spread[p, :, :turns_back], NT, precision=HIGHEST, preferred_element_type=F32
        )
        own = part if own is None else own + part
    hist_src[...] = own
    hist_all[me_b] = own

    loads[0].wait()
    loads[1].wait()
    sums = (lane_sums(0), lane_sums(2))
    pl.semaphore_wait(barrier, n_mp + n_bunch - 2)
    send_sums(0, *sums)
    hist_x.start()
    loads[2].wait()

    iota_c = iota((COARSE, CHUNK), 0)
    iota_f = iota((FINE, CHUNK), 0)
    own_lanes = lax.shift_right_logical(lane8, 5) == (row8 & 3)

    def bin_bunch(ids_ref, source, b):
        acc = None
        for c in range(parts // CHUNK):
            at = pl.ds(c * CHUNK, CHUNK)
            ids = ids_ref[pl.ds(b, 1), at]
            x = source[0, pl.ds(b, 1), at]
            y = source[2, pl.ds(b, 1), at]
            coarse = iota_c == lax.shift_right_logical(ids, 5)
            fine = jnp.where(iota_f == (ids & (FINE - 1)), 1.0, 0.0).astype(BF16)
            rows = [jnp.where(coarse, 1.0, 0.0)]
            for v in (*two_pieces(x), *two_pieces(y)):
                rows.append(jnp.where(coarse, jnp.broadcast_to(v, (COARSE, CHUNK)), 0.0))
            weighted = jnp.concatenate(rows, axis=0).astype(BF16)
            part = lax.dot_general(weighted, fine, NT, preferred_element_type=F32)
            acc = part if acc is None else acc + part
        return acc

    def as_tile(acc):
        tiles = []
        for v in (acc[8:16] + acc[16:24], acc[24:32] + acc[32:40], acc[0:8]):
            v = jnp.where(own_lanes, jnp.concatenate([v] * 4, axis=1), 0.0)
            v = v + pltpu.roll(v, 1, 0)
            tiles.append(v + pltpu.roll(v, 2, 0))
        last = row8 & 3
        tile = jnp.where(
            last == 3,
            tiles[0],
            jnp.where(last == 0, pltpu.roll(tiles[1], 1, 0), pltpu.roll(tiles[2], 2, 0)),
        )
        return tile * scale

    chips, chip = n_mp // 2, lax.div(me_m, 2)
    core = lax.rem(me_m, 2)

    def owner(k):
        u, side = lax.div(k, 2), lax.rem(k, 2)
        reach = chips // 2 - lax.div(u + 1, 2)
        there = lax.rem(chip + reach * (2 * lax.rem(u, 2) - 1) + chips, chips)
        return there * 2 + lax.rem(core + 1 + side, 2)

    def bin_all(turn, ids_ref, source):
        def bin_some(first, count):
            owners = [owner(first + k) for k in range(count)]
            accs = [bin_bunch(ids_ref, source, b) for b in owners]
            return owners, [as_tile(acc) for acc in accs]

        def step(k, _):
            owners, tiles = bin_some(k * AT_ONCE, AT_ONCE)
            for b, tile in zip(owners, tiles):
                msg[turn, b] = tile
            for b in owners:
                msg_copy(turn, b, me_m).start()
            return 0

        lax.fori_loop(0, bunches // AT_ONCE - 1, step, 0)
        owners, tiles = bin_some(bunches - AT_ONCE, AT_ONCE)
        for b, tile in zip(owners[:-1], tiles[:-1]):
            msg[turn, b] = tile
        landed[turn, me_m] = tiles[-1]
        for b in owners[:-1]:
            msg_copy(turn, b, me_m).start()

    def others(act):
        def step(k, _):
            act(lax.rem(me_m + k, n_mp))
            return 0

        lax.fori_loop(1, n_mp, step, 0)

    def toeplitz_rows(r, half, sub):
        d = me_b * bunches + sub * 8 + row8 - (LANES * half + lane8) - 1
        c = d & (SLICES - 1)
        index = c & (LANES - 1)
        low = jnp.broadcast_to(wake_ref[pl.ds(2 * r, 1), :], (8, LANES))
        high = jnp.broadcast_to(wake_ref[pl.ds(2 * r + 1, 1), :], (8, LANES))
        return jnp.where(c >= LANES, gather_lanes(high, index), gather_lanes(low, index)), d >= 0

    def collected(ref):
        halves = []
        for half in range(2):
            total = ref[8 * half]
            for k in range(1, 8):
                total = total + ref[8 * half + k]
            halves.append(total)
        return halves

    def row_of(tile, k):
        return jnp.broadcast_to(tile[k : k + 1, :], (8, LANES))

    def send_far(turn):
        row = lane_row(ext[turn])[:1]
        far_src[turn] = row
        far_all[turn, me_m] = row
        far_x[turn].start()

    def far_first():
        loads[4].wait()
        sum_x[0].arrive()
        hist_x.arrive()
        hist, cent = collected(hist_all), collected(sum_all.at[0])
        kept = jnp.where(me_m == n_mp - 1, 0.0, 1.0)
        for sub in range(2):
            sums = [[jnp.zeros((8, LANES), F32) for _ in range(2)] for _ in range(2)]
            for half in range(2):
                g0, upper = toeplitz_rows(0, half, sub)
                g1, _ = toeplitz_rows(1, half, sub)
                u0 = jnp.where(upper, g0, 0.0)
                u1 = jnp.where(upper, g1, g0)
                toep0[half, pl.ds(8 * sub, 8), :] = u0
                for p in range(2):
                    c = row_of(cent[half], p)
                    sums[0][p] = sums[0][p] + u0 * c
                    sums[1][p] = sums[1][p] + u1 * c
                first = me_m * share
                g = [
                    toeplitz_rows(jnp.minimum(first + k, turns_back), half, sub)[0]
                    for k in range(share + 2)
                ]
                for k in range(share):
                    near = jnp.where(upper, g[k + 1], g[k])
                    later = jnp.where(upper, g[k + 2], g[k + 1])
                    if k == share - 1:
                        later = later * kept
                    for p in range(2):
                        h = row_of(hist[half], p * share + k)
                        sums[0][p] = sums[0][p] + near * h
                        sums[1][p] = sums[1][p] + later * h
            for turn in range(2):
                for p in range(2):
                    ext[turn, pl.ds(p * bunches + 8 * sub, 8), :] = sums[turn][p]
        send_far(0)

    def far_second():
        sum_x[1].arrive()
        cent = collected(sum_all.at[1])
        for sub in range(2):
            for p in range(2):
                at = pl.ds(p * bunches + 8 * sub, 8)
                total = ext[1, at, :]
                for half in range(2):
                    total = total + toep0[half, pl.ds(8 * sub, 8), :] * row_of(cent[half], p)
                ext[1, at, :] = total
        send_far(1)

    def kick_table(turn):
        others(lambda peer: msg_copy(turn, peer, peer).wait_recv())
        total = landed[turn, 0]
        for k in range(1, 16):
            total = total + landed[turn, k]
        wide = jnp.concatenate([total, pltpu.roll(total, 4, 0)], axis=1)
        dip = lax.dot_general(wide, dipole_ref[...], NT, precision=HIGHEST, preferred_element_type=F32)
        quad = lax.dot_general(wide, quad_ref[...], NT, precision=HIGHEST, preferred_element_type=F32)
        moved = jnp.sum(wide, axis=1, keepdims=True)
        low, high = dip[:, :LANES], dip[:, LANES:]
        tab_src[turn] = jnp.concatenate(
            [
                low[3:4],
                high[3:4],
                low[4:5],
                high[4:5],
                quad[5:6, :LANES],
                quad[5:6, LANES:],
                jnp.broadcast_to(moved[3:4], (1, LANES)),
                jnp.broadcast_to(moved[4:5], (1, LANES)),
            ],
            axis=0,
        )
        tab_x[turn].start()
        tab_all[turn, me_m] = tab_src[turn]

    full_row, full_lane = iota((bunches, LANES), 0), iota((bunches, LANES), 1)

    def lay_rows(turn):
        far_x[turn].arrive()
        total = far_all[turn, 0]
        for k in range(1, n_mp):
            total = total + far_all[turn, k]
        total = jnp.broadcast_to(total, (bunches, LANES))
        far = [
            jnp.sum(jnp.where(full_lane == full_row + p * bunches, total, 0.0), axis=1, keepdims=True)
            for p in range(2)
        ]
        tab_x[turn].arrive()

        def column(k):
            return jnp.concatenate([tab_all[turn, n, k : k + 1, :] for n in range(bunches)], axis=0)

        for k in range(6):
            row = column(k)
            rows_ref[k] = row + far[k // 2] if k < 4 else row
        for p in range(2):
            spot = jnp.where(full_row == full_lane, column(6 + p), 0.0)
            cent_ref[p, turn : turn + 1, :] = jnp.sum(spot, axis=0, keepdims=True)[:, :bunches]

    bin_all(0, first_ids, phase_ref)
    far_first()

    loads[5].wait()
    for p in range(2):
        wide = jnp.concatenate([advance_ref[p : p + 1, :], jnp.zeros((1, LANES - bunches), F32)], axis=1)
        wide = jnp.broadcast_to(wide, (bunches, LANES))
        column = jnp.sum(jnp.where(full_row == full_lane, wide, 0.0), axis=1, keepdims=True)
        sin, cos = sin_cos(jnp.broadcast_to(column, (bunches, LANES)))
        rot[2 * p] = cos
        rot[2 * p + 1] = sin

    loads[6].wait()
    loads[7].wait()
    kick_table(0)
    loads[8].wait()
    loads[9].wait()
    loads[10].wait()
    lay_rows(0)

    sums = []
    for g in range(bunches // GROUP):
        at = pl.ds(g * GROUP, GROUP)
        rows = [rows_ref[k, at, :] for k in range(6)]
        turn_by = [rot[k, at, :] for k in range(4)]

        def kick(c, acc):
            lanes = pl.ds(pl.multiple_of(c * WIDTH, WIDTH), WIDTH)
            new = turned(first_ids[at, lanes], [phase_ref[k, at, lanes] for k in range(4)], rows, turn_by)
            for k in range(4):
                mid_ref[k, at, lanes] = new[k]
            acc = list(acc)
            for s in range(WIDTH // LANES):
                cut = slice(s * LANES, (s + 1) * LANES)
                acc = [acc[0] + new[0][:, cut], acc[1] + new[2][:, cut]]
            return tuple(acc)

        zero = jnp.zeros((GROUP, LANES), F32)
        sums.append(lax.fori_loop(0, parts // WIDTH, kick, (zero, zero)))
    send_sums(1, *(jnp.concatenate([s[p] for s in sums], axis=0) for p in range(2)))

    bin_all(1, next_ids, mid_ref)
    kick_table(1)
    far_second()
    lay_rows(1)

    for turn in range(TURNS):
        others(lambda peer: msg_copy(turn, peer, me_m).wait_send())
        for exchange in (tab_x[turn], far_x[turn], sum_x[turn]):
            exchange.leave()
    hist_x.leave()


def last_kernel(mid_ref, ids_ref, rows_ref, rot, cent_in, out_hbm, cent_hbm, out_ref, cent_ref, sems):
    bunches, parts = mid_ref.shape[1], mid_ref.shape[2]
    cent_ref[...] = cent_in[...]
    copies = [pltpu.make_async_copy(cent_ref, cent_hbm, sems.at[0])]
    copies[0].start()
    span = parts // SPANS
    for g in range(bunches // GROUP):
        at = pl.ds(g * GROUP, GROUP)
        rows = [rows_ref[k, at, :] for k in range(6)]
        turn_by = [rot[k, at, :] for k in range(4)]
        for part in range(SPANS):

            def kick(c, _):
                lanes = pl.ds(pl.multiple_of(part * span + c * WIDTH, WIDTH), WIDTH)
                new = turned(ids_ref[at, lanes], [mid_ref[k, at, lanes] for k in range(4)], rows, turn_by)
                for k in range(4):
                    out_ref[k, at, lanes] = new[k]
                return 0

            lax.fori_loop(0, span // WIDTH, kick, 0)
            block = (slice(None), at, pl.ds(part * span, span))
            copies.append(
                pltpu.make_async_copy(out_ref.at[block], out_hbm.at[block], sems.at[len(copies)])
            )
            copies[-1].start()
    for copy in copies:
        copy.wait()


def body(phase_space, phase_advance, centroid_history, lr_wake, sr_dipole, sr_quad, slice_ids):
    n_bunch, n_mp = lax.axis_size("bunch"), lax.axis_size("mp")
    bunches, parts = phase_space.shape[1:]
    turns_back = centroid_history.shape[1]
    wake_rows = lr_wake.shape[0] // LANES
    vmem, hbm = pl.BlockSpec(memory_space=pltpu.VMEM), pl.BlockSpec(memory_space=pltpu.HBM)
    dma = pltpu.SemaphoreType.DMA

    def held(*shape, dtype=F32):
        return pltpu.VMEM(shape, dtype)

    cent_shape = jax.ShapeDtypeStruct((2, TURNS, bunches), F32)
    state = pl.pallas_call(
        functools.partial(track_kernel, (n_bunch, n_mp)),
        out_shape=(
            jax.ShapeDtypeStruct(phase_space.shape, F32),
            jax.ShapeDtypeStruct((bunches, parts), I32),
            jax.ShapeDtypeStruct((6, bunches, LANES), F32),
            jax.ShapeDtypeStruct((4, bunches, LANES), F32),
            cent_shape,
        ),
        in_specs=[hbm] * 7,
        out_specs=(vmem,) * 5,
        scratch_shapes=[
            held(4, bunches, parts),
            held(bunches, parts, dtype=I32),
            held(2, bunches),
            held(2, bunches, turns_back),
            held(wake_rows, LANES),
            held(SLICES, SLICES),
            held(SLICES, SLICES),
            held(TURNS, bunches, 8, LANES),
            held(TURNS, n_mp, 8, LANES),
            held(8, LANES),
            held(n_bunch, 8, LANES),
            held(TURNS, 2, LANES),
            held(TURNS, n_bunch, 2, LANES),
            held(TURNS, 1, LANES),
            held(TURNS, n_mp, 1, LANES),
            held(TURNS, 8, LANES),
            held(TURNS, n_mp, 8, LANES),
            held(2, LANES, LANES),
            held(TURNS, LANES, LANES),
            held(2, bunches, LANES),
            dma((11,)),
            dma((TURNS, n_mp)),
            dma((TURNS, n_mp)),
            dma((n_bunch,)),
            dma((n_bunch,)),
            dma((TURNS, n_bunch)),
            dma((TURNS, n_bunch)),
            dma((TURNS, n_mp)),
            dma((TURNS, n_mp)),
            dma((TURNS, n_mp)),
            dma((TURNS, n_mp)),
        ],
        compiler_params=pltpu.CompilerParams(
            collective_id=0, has_side_effects=True, vmem_limit_bytes=40 << 20
        ),
        cost_estimate=pl.CostEstimate(flops=4 * 65536 * 256, bytes_accessed=3 << 20, transcendentals=0),
        name="track",
    )(
        *(
            pltpu.with_memory_space_constraint(a, pltpu.HBM)
            for a in (
                phase_space,
                phase_advance,
                jnp.transpose(centroid_history, (0, 2, 1)),
                lr_wake.reshape(-1, LANES),
                sr_dipole,
                sr_quad,
                slice_ids,
            )
        )
    )
    return tuple(
        pl.pallas_call(
            last_kernel,
            out_shape=(jax.ShapeDtypeStruct(phase_space.shape, F32), cent_shape),
            in_specs=[vmem] * 5,
            out_specs=(hbm, hbm),
            scratch_shapes=[
                held(*phase_space.shape),
                held(2, TURNS, bunches),
                dma((1 + SPANS * bunches // GROUP,)),
            ],
            compiler_params=pltpu.CompilerParams(vmem_limit_bytes=16 << 20),
            cost_estimate=pl.CostEstimate(flops=100 * 65536, bytes_accessed=1 << 20, transcendentals=0),
            name="last",
        )(*state)
    )


def solution(mesh):
    placed = (
        P(None, "bunch", "mp"),
        P(None, "bunch"),
        P(None, None, "bunch"),
        P(),
        P(),
        P(),
        P(None, "bunch", "mp"),
    )
    return jax.shard_map(
        body,
        mesh=mesh,
        in_specs=placed,
        out_specs=(P(None, "bunch", "mp"), P(None, None, "bunch")),
        check_vma=False,
    )
```

time: 58.7 us -> 46.8 us (0.80)
  local copies, waits for them, and re-layouts: 6.58 us -> 0 us
  Pallas kernels: 51.2 us -> 46.1 us
    unnamed x15 -> x0, local copies, waits for them, and re-layouts: 6.58 us -> none
    pallas_call x1 -> x2, Pallas kernels: 51.2 us -> 46.1 us  [the longest x1 42.7 us: body(): pl.pallas_call(functools.partial(track_kernel, (n_bunch, n_mp)), out_shap...]
where the time goes in v2:
time: 46.8 us; the launch traced here: 46.7 us
  Pallas kernels  46.1 us (99%)
  between operations  0.64 us (1%)
    pallas_call x1, Pallas kernels, body(): pl.pallas_call(functools.partial(track_kernel, (n_bunch, n_mp)), out_shap...  42.7 us
    pallas_call x1, Pallas kernels, body(): pl.pallas_call(last_kernel, out_shape=(jax.ShapeDtypeStruct(phase_space.s...  3.37 us

profile of v2, /device:TPU:1, one launch (start us, length us, event | category | flops | bytes accessed | tf_op | source)
XLA Modules:
  0.0 46.7 jit_solution(7321282899142477410)
XLA Ops:
  0.6 42.7 %track.1 = (f32[4,16,4096]{2,1,0:T(8,128)S(1)}, s32[16,4096]{1,0:T(8,128)S(1)}, f32[6,16,128]{2,1,0:T(8,128)S(1)}, f32[4,16,128]{2,1,0:T(8,128)S(1)}, f32[2,2,16]{2,1,0:T(2,128)S(1)}) custom-call(f32[4,16,4096]{2,1,0:T(8,128)} %phase_hbm.1, f32[2,16]{1,0:T(2,128)} %advance_hbm.1, f32[2,16,64]{2,1,0:T(8,128)} %bitcast.3, f32[130,128]{1,0:T(8,128)} %bitcast.2, ...), custom_call_target="tpu_custom_call" | custom-call | flops 67108864 | bytes 3145728 | tf_op jit(solution)/shard_map/track/pallas_call | solution.py:557
  43.4 3.4 %last.1 = (f32[4,16,4096]{2,1,0:T(8,128)}, f32[2,2,16]{2,1,0:T(2,128)}) custom-call(f32[4,16,4096]{2,1,0:T(8,128)S(1)} %get-tuple-element.7.mid_ref, s32[16,4096]{1,0:T(8,128)S(1)} %get-tuple-element.8.ids_ref, f32[6,16,128]{2,1,0:T(8,128)S(1)} %get-tuple-element.9.rows_ref, f32[4,16,128]{2,1,0:T(8,128)S(1)} %get-tuple-element.10.rot, ...), custom_call_target="tpu_custom_call" | custom-call | flops 6553600 | bytes 1048576 | tf_op jit(solution)/shard_map/last/pallas_call | solution.py:621

commit v3 on v2

--- a/solution.py
+++ b/solution.py
@@ -14,7 +14,7 @@
 COARSE, FINE = 8, 32
 CHUNK = 512
 GROUP = 8
-AT_ONCE = 4
+AT_ONCE = 8
 WIDTH = 512
 SPANS = 2
 
@@ -112,9 +112,8 @@
     far_all,
     tab_src,
     tab_all,
-    spread,
     ext,
-    toep0,
+    toep,
     load,
     msg_send,
     msg_recv,
@@ -164,72 +163,89 @@
     for copy in loads:
         copy.start()
 
+    def by_reach(n, step):
+        return sorted(range(1, n), key=lambda k: -min(k // step, (n - k) // step))
+
     class Exchange:
-        def __init__(self, axis, me, n, source, target, send, recv):
-            self.axis, self.me, self.n = axis, me, n
+        def __init__(self, axis, me, offsets, source, target, send, recv):
+            self.axis, self.me, self.offsets = axis, me, offsets
             self.source, self.target, self.send, self.recv = source, target, send, recv
 
-        def copy(self, peer, slot):
+        def start(self):
+            for k in self.offsets:
+                pltpu.make_async_remote_copy(
+                    src_ref=self.source,
+                    dst_ref=self.target.at[self.me],
+                    send_sem=self.send,
+                    recv_sem=self.recv,
+                    device_id={self.axis: lax.rem(self.me + k, len(self.offsets) + 1)},
+                ).start()
+
+        def all_of_them(self):
+            block = self.target.at[pl.ds(0, len(self.offsets))]
             return pltpu.make_async_remote_copy(
-                src_ref=self.source,
-                dst_ref=self.target.at[slot],
-                send_sem=self.send.at[peer],
-                recv_sem=self.recv.at[slot],
-                device_id={self.axis: peer},
+                src_ref=block,
+                dst_ref=block,
+                send_sem=self.send,
+                recv_sem=self.recv,
+                device_id={self.axis: lax.rem(self.me + 1, len(self.offsets) + 1)},
             )
 
-        def each(self, act):
-            def step(k, _):
-                act(lax.rem(self.me + lax.rem(k + self.n // 2 - 1, self.n - 1) + 1, self.n))
-                return 0
-
-            lax.fori_loop(0, self.n - 1, step, 0)
-
-        def start(self):
-            self.each(lambda peer: self.copy(peer, self.me).start())
-
         def arrive(self):
-            self.each(lambda peer: self.copy(peer, peer).wait_recv())
+            self.all_of_them().wait_recv()
 
         def leave(self):
-            self.each(lambda peer: self.copy(peer, self.me).wait_send())
-
-    hist_x = Exchange("bunch", me_b, n_bunch, hist_src, hist_all, hist_send, hist_recv)
+            self.all_of_them().wait_send()
+
+    across, along = by_reach(n_bunch, 1), by_reach(n_mp, 2)
+    hist_x = Exchange("bunch", me_b, across, hist_src, hist_all, hist_send, hist_recv)
     sum_x = [
-        Exchange("bunch", me_b, n_bunch, sum_src.at[t], sum_all.at[t], sum_send.at[t], sum_recv.at[t])
+        Exchange("bunch", me_b, across, sum_src.at[t], sum_all.at[t], sum_send.at[t], sum_recv.at[t])
         for t in range(TURNS)
     ]
     far_x = [
-        Exchange("mp", me_m, n_mp, far_src.at[t], far_all.at[t], far_send.at[t], far_recv.at[t])
+        Exchange("mp", me_m, along, far_src.at[t], far_all.at[t], far_send.at[t], far_recv.at[t])
         for t in range(TURNS)
     ]
     tab_x = [
-        Exchange("mp", me_m, n_mp, tab_src.at[t], tab_all.at[t], tab_send.at[t], tab_recv.at[t])
+        Exchange("mp", me_m, along, tab_src.at[t], tab_all.at[t], tab_send.at[t], tab_recv.at[t])
         for t in range(TURNS)
     ]
-
-    def msg_copy(turn, b, slot):
-        return pltpu.make_async_remote_copy(
+    msg_x = [
+        Exchange("mp", me_m, along, None, landed.at[t], msg_send.at[t], msg_recv.at[t]) for t in range(TURNS)
+    ]
+
+    def send_msg(turn, b):
+        pltpu.make_async_remote_copy(
             src_ref=msg.at[turn, b],
-            dst_ref=landed.at[turn, slot],
-            send_sem=msg_send.at[turn, b],
-            recv_sem=msg_recv.at[turn, slot],
+            dst_ref=landed.at[turn, me_m],
+            send_sem=msg_send.at[turn],
+            recv_sem=msg_recv.at[turn],
             device_id={"mp": b},
-        )
+        ).start()
 
     row8, lane8 = iota((8, LANES), 0), iota((8, LANES), 1)
     place = lax.rem(me_b, 8) * bunches
-    ones = jnp.ones((8, LANES), F32)
-
-    def lane_row(block):
-        return lax.dot_general(ones, block, NT, precision=HIGHEST, preferred_element_type=F32)
-
-    spread[...] = jnp.zeros_like(spread)
+
+    def pieces(block):
+        parts = []
+        for _ in range(3):
+            parts.append(block.astype(BF16))
+            block = block - parts[-1].astype(F32)
+        return jnp.concatenate(parts, axis=1)
+
+    def to_lanes(chosen, block):
+        rows = lax.dot_general(
+            jnp.concatenate([chosen.astype(BF16)] * 3, axis=1), pieces(block), NT, preferred_element_type=F32
+        )
+        return jnp.concatenate([rows, jnp.zeros((16, LANES - block.shape[0]), F32)], axis=1)
 
     def send_sums(turn, sums_x, sums_y):
-        spread[0, pl.ds(place, bunches), :] = sums_x * scale
-        spread[1, pl.ds(place, bunches), :] = sums_y * scale
-        rows = jnp.concatenate([lane_row(spread[0])[:1], lane_row(spread[1])[:1]], axis=0)
+        both = to_lanes(jnp.ones((16, LANES), F32), jnp.concatenate([sums_x, sums_y], axis=0) * scale)[:8]
+        x = pltpu.roll(jnp.where(lane8 < bunches, both, 0.0), place, 1)
+        y = jnp.where((lane8 >= bunches) & (lane8 < 2 * bunches), both, 0.0)
+        y = pltpu.roll(y, lax.rem(place + LANES - bunches, LANES), 1)
+        rows = jnp.where(row8 == 0, x, y)[:2]
         sum_src[turn] = rows
         sum_all[turn, me_b] = rows
         sum_x[turn].start()
@@ -240,26 +256,18 @@
 
         return lax.fori_loop(0, parts // LANES, step, jnp.zeros((bunches, LANES), F32), unroll=8)
 
-    loads[3].wait()
-    pick = iota((8, turns_back), 1) == me_m * share + (iota((8, turns_back), 0) & (share - 1))
-    halves = iota((8, turns_back), 0) < share
-    own = None
-    for p in range(2):
-        spread[p, pl.ds(place, bunches), :turns_back] = hist_ref[p]
-        chosen = jnp.where(pick & (halves if p == 0 else ~halves), 1.0, 0.0)
-        part = lax.dot_general(
-            chosen, spread[p, :, :turns_back], NT, precision=HIGHEST, preferred_element_type=F32
-        )
-        own = part if own is None else own + part
-    hist_src[...] = own
-    hist_all[me_b] = own
+    def send_history():
+        loads[3].wait()
+        r, c = iota((16, 2 * turns_back), 0), iota((16, 2 * turns_back), 1)
+        chosen = jnp.where(c == (r // share) * turns_back + me_m * share + (r & (share - 1)), 1.0, 0.0)
+        own = to_lanes(chosen, jnp.concatenate([hist_ref[0], hist_ref[1]], axis=1))[:8]
+        own = pltpu.roll(own, place, 1)
+        hist_src[...] = own
+        hist_all[me_b] = own
+        hist_x.start()
 
     loads[0].wait()
     loads[1].wait()
-    sums = (lane_sums(0), lane_sums(2))
-    pl.semaphore_wait(barrier, n_mp + n_bunch - 2)
-    send_sums(0, *sums)
-    hist_x.start()
     loads[2].wait()
 
     iota_c = iota((COARSE, CHUNK), 0)
@@ -301,39 +309,24 @@
     core = lax.rem(me_m, 2)
 
     def owner(k):
-        u, side = lax.div(k, 2), lax.rem(k, 2)
-        reach = chips // 2 - lax.div(u + 1, 2)
-        there = lax.rem(chip + reach * (2 * lax.rem(u, 2) - 1) + chips, chips)
+        u, side = k // 2, k % 2
+        reach = (chips // 2 - (u + 1) // 2) * (2 * (u % 2) - 1)
+        there = lax.rem(chip + reach + chips, chips)
         return there * 2 + lax.rem(core + 1 + side, 2)
 
-    def bin_all(turn, ids_ref, source):
-        def bin_some(first, count):
-            owners = [owner(first + k) for k in range(count)]
-            accs = [bin_bunch(ids_ref, source, b) for b in owners]
-            return owners, [as_tile(acc) for acc in accs]
-
-        def step(k, _):
-            owners, tiles = bin_some(k * AT_ONCE, AT_ONCE)
+    def bin_all(turn, ids_ref, source, between):
+        for first in range(0, bunches, AT_ONCE):
+            owners = [owner(first + k) for k in range(AT_ONCE)]
+            tiles = [as_tile(bin_bunch(ids_ref, source, b)) for b in owners]
+            if first == 0:
+                between()
+            if first + AT_ONCE == bunches:
+                landed[turn, me_m] = tiles[-1]
+                owners = owners[:-1]
             for b, tile in zip(owners, tiles):
                 msg[turn, b] = tile
             for b in owners:
-                msg_copy(turn, b, me_m).start()
-            return 0
-
-        lax.fori_loop(0, bunches // AT_ONCE - 1, step, 0)
-        owners, tiles = bin_some(bunches - AT_ONCE, AT_ONCE)
-        for b, tile in zip(owners[:-1], tiles[:-1]):
-            msg[turn, b] = tile
-        landed[turn, me_m] = tiles[-1]
-        for b in owners[:-1]:
-            msg_copy(turn, b, me_m).start()
-
-    def others(act):
-        def step(k, _):
-            act(lax.rem(me_m + k, n_mp))
-            return 0
-
-        lax.fori_loop(1, n_mp, step, 0)
+                send_msg(turn, b)
 
     def toeplitz_rows(r, half, sub):
         d = me_b * bunches + sub * 8 + row8 - (LANES * half + lane8) - 1
@@ -356,42 +349,49 @@
         return jnp.broadcast_to(tile[k : k + 1, :], (8, LANES))
 
     def send_far(turn):
-        row = lane_row(ext[turn])[:1]
+        row = to_lanes(jnp.ones((16, LANES), F32), ext[turn])[:1]
         far_src[turn] = row
         far_all[turn, me_m] = row
         far_x[turn].start()
 
-    def far_first():
+    def lay_wake():
         loads[4].wait()
-        sum_x[0].arrive()
-        hist_x.arrive()
-        hist, cent = collected(hist_all), collected(sum_all.at[0])
         kept = jnp.where(me_m == n_mp - 1, 0.0, 1.0)
+        first = me_m * share
         for sub in range(2):
-            sums = [[jnp.zeros((8, LANES), F32) for _ in range(2)] for _ in range(2)]
+            at = pl.ds(8 * sub, 8)
             for half in range(2):
                 g0, upper = toeplitz_rows(0, half, sub)
                 g1, _ = toeplitz_rows(1, half, sub)
-                u0 = jnp.where(upper, g0, 0.0)
-                u1 = jnp.where(upper, g1, g0)
-                toep0[half, pl.ds(8 * sub, 8), :] = u0
-                for p in range(2):
-                    c = row_of(cent[half], p)
-                    sums[0][p] = sums[0][p] + u0 * c
-                    sums[1][p] = sums[1][p] + u1 * c
-                first = me_m * share
+                toep[0, half, at, :] = jnp.where(upper, g0, 0.0)
+                toep[1, half, at, :] = jnp.where(upper, g1, g0)
                 g = [
                     toeplitz_rows(jnp.minimum(first + k, turns_back), half, sub)[0]
                     for k in range(share + 2)
                 ]
+                for k in range(share + 1):
+                    near = jnp.where(upper, g[k + 1], g[k])
+                    toep[2 + k, half, at, :] = near
+                toep[2 + share + 1, half, at, :] = near * kept
+
+    def far_first():
+        sum_x[0].arrive()
+        hist_x.arrive()
+        hist, cent = collected(hist_all), collected(sum_all.at[0])
+        for sub in range(2):
+            at = pl.ds(8 * sub, 8)
+            sums = [[jnp.zeros((8, LANES), F32) for _ in range(2)] for _ in range(2)]
+            for half in range(2):
+                u = [toep[k, half, at, :] for k in range(share + 4)]
+                for p in range(2):
+                    c = row_of(cent[half], p)
+                    sums[0][p] = sums[0][p] + u[0] * c
+                    sums[1][p] = sums[1][p] + u[1] * c
                 for k in range(share):
-                    near = jnp.where(upper, g[k + 1], g[k])
-                    later = jnp.where(upper, g[k + 2], g[k + 1])
-                    if k == share - 1:
-                        later = later * kept
                     for p in range(2):
                         h = row_of(hist[half], p * share + k)
-                        sums[0][p] = sums[0][p] + near * h
+                        sums[0][p] = sums[0][p] + u[2 + k] * h
+                        later = u[3 + k] if k < share - 1 else u[3 + share]
                         sums[1][p] = sums[1][p] + later * h
             for turn in range(2):
                 for p in range(2):
@@ -406,12 +406,12 @@
                 at = pl.ds(p * bunches + 8 * sub, 8)
                 total = ext[1, at, :]
                 for half in range(2):
-                    total = total + toep0[half, pl.ds(8 * sub, 8), :] * row_of(cent[half], p)
+                    total = total + toep[0, half, pl.ds(8 * sub, 8), :] * row_of(cent[half], p)
                 ext[1, at, :] = total
         send_far(1)
 
     def kick_table(turn):
-        others(lambda peer: msg_copy(turn, peer, peer).wait_recv())
+        msg_x[turn].arrive()
         total = landed[turn, 0]
         for k in range(1, 16):
             total = total + landed[turn, k]
@@ -460,8 +460,13 @@
             spot = jnp.where(full_row == full_lane, column(6 + p), 0.0)
             cent_ref[p, turn : turn + 1, :] = jnp.sum(spot, axis=0, keepdims=True)[:, :bunches]
 
-    bin_all(0, first_ids, phase_ref)
-    far_first()
+    def first_sends():
+        pl.semaphore_wait(barrier, n_mp + n_bunch - 2)
+        send_sums(0, lane_sums(0), lane_sums(2))
+        send_history()
+
+    bin_all(0, first_ids, phase_ref, first_sends)
+    lay_wake()
 
     loads[5].wait()
     for p in range(2):
@@ -475,6 +480,7 @@
     loads[6].wait()
     loads[7].wait()
     kick_table(0)
+    far_first()
     loads[8].wait()
     loads[9].wait()
     loads[10].wait()
@@ -498,17 +504,16 @@
             return tuple(acc)
 
         zero = jnp.zeros((GROUP, LANES), F32)
-        sums.append(lax.fori_loop(0, parts // WIDTH, kick, (zero, zero)))
+        sums.append(lax.fori_loop(0, parts // WIDTH, kick, (zero, zero), unroll=4))
     send_sums(1, *(jnp.concatenate([s[p] for s in sums], axis=0) for p in range(2)))
 
-    bin_all(1, next_ids, mid_ref)
+    bin_all(1, next_ids, mid_ref, lambda: None)
     kick_table(1)
     far_second()
     lay_rows(1)
 
     for turn in range(TURNS):
-        others(lambda peer: msg_copy(turn, peer, me_m).wait_send())
-        for exchange in (tab_x[turn], far_x[turn], sum_x[turn]):
+        for exchange in (msg_x[turn], tab_x[turn], far_x[turn], sum_x[turn]):
             exchange.leave()
     hist_x.leave()
 
@@ -532,7 +537,7 @@
                     out_ref[k, at, lanes] = new[k]
                 return 0
 
-            lax.fori_loop(0, span // WIDTH, kick, 0)
+            lax.fori_loop(0, span // WIDTH, kick, 0, unroll=4)
             block = (slice(None), at, pl.ds(part * span, span))
             copies.append(
                 pltpu.make_async_copy(out_ref.at[block], out_hbm.at[block], sems.at[len(copies)])
@@ -583,20 +588,19 @@
             held(TURNS, n_mp, 1, LANES),
             held(TURNS, 8, LANES),
             held(TURNS, n_mp, 8, LANES),
-            held(2, LANES, LANES),
-            held(TURNS, LANES, LANES),
-            held(2, bunches, LANES),
+            held(TURNS, 2 * bunches, LANES),
+            held(4 + turns_back // n_mp, 2, bunches, LANES),
             dma((11,)),
-            dma((TURNS, n_mp)),
-            dma((TURNS, n_mp)),
-            dma((n_bunch,)),
-            dma((n_bunch,)),
-            dma((TURNS, n_bunch)),
-            dma((TURNS, n_bunch)),
-            dma((TURNS, n_mp)),
-            dma((TURNS, n_mp)),
-            dma((TURNS, n_mp)),
-            dma((TURNS, n_mp)),
+            dma((TURNS,)),
+            dma((TURNS,)),
+            dma,
+            dma,
+            dma((TURNS,)),
+            dma((TURNS,)),
+            dma((TURNS,)),
+            dma((TURNS,)),
+            dma((TURNS,)),
+            dma((TURNS,)),
         ],
         compiler_params=pltpu.CompilerParams(
             collective_id=0, has_side_effects=True, vmem_limit_bytes=40 << 20

time: 46.8 us -> 37.9 us (0.81)
  Pallas kernels: 46.1 us -> 37.1 us
    pallas_call x1, Pallas kernels: 42.7 us -> 35.3 us  [body(): pl.pallas_call(functools.partial(track_kernel, (n_bunch, n_mp)), out_shap...]
    pallas_call x1, Pallas kernels: 3.37 us -> 1.79 us  [body(): pl.pallas_call(last_kernel, out_shape=(jax.ShapeDtypeStruct(phase_space.s...]
where the time goes in v3:
time: 37.9 us; the launch traced here: 37.8 us
  Pallas kernels  37.1 us (98%)
  between operations  0.64 us (2%)
    pallas_call x1, Pallas kernels, body(): pl.pallas_call(functools.partial(track_kernel, (n_bunch, n_mp)), out_shap...  35.3 us
    pallas_call x1, Pallas kernels, body(): pl.pallas_call(last_kernel, out_shape=(jax.ShapeDtypeStruct(phase_space.s...  1.79 us

profile of v3, /device:TPU:1, one launch (start us, length us, event | category | flops | bytes accessed | tf_op | source)
XLA Modules:
  0.0 37.8 jit_solution(5569433131154127461)
XLA Ops:
  0.6 35.3 %track.1 = (f32[4,16,4096]{2,1,0:T(8,128)S(1)}, s32[16,4096]{1,0:T(8,128)S(1)}, f32[6,16,128]{2,1,0:T(8,128)S(1)}, f32[4,16,128]{2,1,0:T(8,128)S(1)}, f32[2,2,16]{2,1,0:T(2,128)S(1)}) custom-call(f32[4,16,4096]{2,1,0:T(8,128)} %phase_hbm.1, f32[2,16]{1,0:T(2,128)} %advance_hbm.1, f32[2,16,64]{2,1,0:T(8,128)} %bitcast.3, f32[130,128]{1,0:T(8,128)} %bitcast.2, ...), custom_call_target="tpu_custom_call" | custom-call | flops 67108864 | bytes 3145728 | tf_op jit(solution)/shard_map/track/pallas_call | solution.py:562
  36.0 1.8 %last.1 = (f32[4,16,4096]{2,1,0:T(8,128)}, f32[2,2,16]{2,1,0:T(2,128)}) custom-call(f32[4,16,4096]{2,1,0:T(8,128)S(1)} %get-tuple-element.7.mid_ref, s32[16,4096]{1,0:T(8,128)S(1)} %get-tuple-element.8.ids_ref, f32[6,16,128]{2,1,0:T(8,128)S(1)} %get-tuple-element.9.rows_ref, f32[4,16,128]{2,1,0:T(8,128)S(1)} %get-tuple-element.10.rot, ...), custom_call_target="tpu_custom_call" | custom-call | flops 6553600 | bytes 1048576 | tf_op jit(solution)/shard_map/last/pallas_call | solution.py:625

commit v4 on v3

--- a/solution.py
+++ b/solution.py
@@ -114,6 +114,8 @@
     tab_all,
     ext,
     toep,
+    partial,
+    split,
     load,
     msg_send,
     msg_recv,
@@ -132,15 +134,6 @@
     turns_back = hist_ref.shape[2]
     share = turns_back // n_mp
     scale = 1.0 / (parts * n_mp)
-
-    barrier = pltpu.get_barrier_semaphore()
-
-    def greet(k, _):
-        pl.semaphore_signal(barrier, inc=1, device_id={"mp": lax.rem(me_m + k, n_mp)})
-        pl.semaphore_signal(barrier, inc=1, device_id={"bunch": lax.rem(me_b + k, n_bunch)})
-        return 0
-
-    lax.fori_loop(1, 16, greet, 0)
 
     loads = [
         pltpu.make_async_copy(source, target, load.at[k])
@@ -163,6 +156,12 @@
     for copy in loads:
         copy.start()
 
+    barrier = pltpu.get_barrier_semaphore()
+    for k in range(1, n_mp):
+        pl.semaphore_signal(barrier, inc=1, device_id={"mp": lax.rem(me_m + k, n_mp)})
+    for k in range(1, n_bunch):
+        pl.semaphore_signal(barrier, inc=1, device_id={"bunch": lax.rem(me_b + k, n_bunch)})
+
     def by_reach(n, step):
         return sorted(range(1, n), key=lambda k: -min(k // step, (n - k) // step))
 
@@ -242,6 +241,7 @@
 
     def send_sums(turn, sums_x, sums_y):
         both = to_lanes(jnp.ones((16, LANES), F32), jnp.concatenate([sums_x, sums_y], axis=0) * scale)[:8]
+        partial[turn] = pltpu.roll(both, 2 * bunches, 1)[:1]
         x = pltpu.roll(jnp.where(lane8 < bunches, both, 0.0), place, 1)
         y = jnp.where((lane8 >= bunches) & (lane8 < 2 * bunches), both, 0.0)
         y = pltpu.roll(y, lax.rem(place + LANES - bunches, LANES), 1)
@@ -272,7 +272,7 @@
 
     iota_c = iota((COARSE, CHUNK), 0)
     iota_f = iota((FINE, CHUNK), 0)
-    own_lanes = lax.shift_right_logical(lane8, 5) == (row8 & 3)
+    own_lanes = lax.shift_right_logical(lane8, 5) == lax.shift_right_logical(row8, 1)
 
     def bin_bunch(ids_ref, source, b):
         acc = None
@@ -281,7 +281,7 @@
             ids = ids_ref[pl.ds(b, 1), at]
             x = source[0, pl.ds(b, 1), at]
             y = source[2, pl.ds(b, 1), at]
-            coarse = iota_c == lax.shift_right_logical(ids, 5)
+            coarse = iota_c == ((lax.shift_right_logical(ids, 4) & 6) | lax.shift_right_logical(ids, 7))
             fine = jnp.where(iota_f == (ids & (FINE - 1)), 1.0, 0.0).astype(BF16)
             rows = [jnp.where(coarse, 1.0, 0.0)]
             for v in (*two_pieces(x), *two_pieces(y)):
@@ -295,15 +295,10 @@
         tiles = []
         for v in (acc[8:16] + acc[16:24], acc[24:32] + acc[32:40], acc[0:8]):
             v = jnp.where(own_lanes, jnp.concatenate([v] * 4, axis=1), 0.0)
-            v = v + pltpu.roll(v, 1, 0)
-            tiles.append(v + pltpu.roll(v, 2, 0))
-        last = row8 & 3
-        tile = jnp.where(
-            last == 3,
-            tiles[0],
-            jnp.where(last == 0, pltpu.roll(tiles[1], 1, 0), pltpu.roll(tiles[2], 2, 0)),
-        )
-        return tile * scale
+            v = v + pltpu.roll(v, 2, 0)
+            tiles.append(v + pltpu.roll(v, 4, 0))
+        tile = jnp.where(row8 < 2, tiles[0], jnp.where(row8 < 4, tiles[1], tiles[2]))
+        return (tile * scale)[:6]
 
     chips, chip = n_mp // 2, lax.div(me_m, 2)
     core = lax.rem(me_m, 2)
@@ -314,12 +309,12 @@
         there = lax.rem(chip + reach + chips, chips)
         return there * 2 + lax.rem(core + 1 + side, 2)
 
-    def bin_all(turn, ids_ref, source, between):
+    def bin_all(turn, ids_ref, source, before, after):
         for first in range(0, bunches, AT_ONCE):
             owners = [owner(first + k) for k in range(AT_ONCE)]
             tiles = [as_tile(bin_bunch(ids_ref, source, b)) for b in owners]
             if first == 0:
-                between()
+                before()
             if first + AT_ONCE == bunches:
                 landed[turn, me_m] = tiles[-1]
                 owners = owners[:-1]
@@ -327,6 +322,8 @@
                 msg[turn, b] = tile
             for b in owners:
                 send_msg(turn, b)
+            if first == 0:
+                after()
 
     def toeplitz_rows(r, half, sub):
         d = me_b * bunches + sub * 8 + row8 - (LANES * half + lane8) - 1
@@ -349,7 +346,7 @@
         return jnp.broadcast_to(tile[k : k + 1, :], (8, LANES))
 
     def send_far(turn):
-        row = to_lanes(jnp.ones((16, LANES), F32), ext[turn])[:1]
+        row = to_lanes(jnp.ones((16, LANES), F32), ext[turn])[:1] + partial[turn]
         far_src[turn] = row
         far_all[turn, me_m] = row
         far_x[turn].start()
@@ -415,23 +412,27 @@
         total = landed[turn, 0]
         for k in range(1, 16):
             total = total + landed[turn, k]
-        wide = jnp.concatenate([total, pltpu.roll(total, 4, 0)], axis=1)
-        dip = lax.dot_general(wide, dipole_ref[...], NT, precision=HIGHEST, preferred_element_type=F32)
-        quad = lax.dot_general(wide, quad_ref[...], NT, precision=HIGHEST, preferred_element_type=F32)
-        moved = jnp.sum(wide, axis=1, keepdims=True)
+        total = jnp.concatenate([total, jnp.zeros((2, LANES), F32)], axis=0)
+        wide = jnp.concatenate([total, pltpu.roll(total, 7, 0)], axis=1)
+        stack = []
+        for _ in range(3):
+            stack.append(wide.astype(BF16).astype(F32))
+            wide = wide - stack[-1]
+        stack = jnp.concatenate(stack, axis=0).astype(BF16)
+
+        def product(which):
+            out = None
+            for k in reversed(range(3)):
+                part = jnp.dot(stack, split[which, k], preferred_element_type=F32)
+                for n in reversed(range(3 - k)):
+                    block = part[8 * n : 8 * n + 8]
+                    out = block if out is None else out + block
+            return out
+
+        dip, quad = product(0), product(1)
         low, high = dip[:, :LANES], dip[:, LANES:]
         tab_src[turn] = jnp.concatenate(
-            [
-                low[3:4],
-                high[3:4],
-                low[4:5],
-                high[4:5],
-                quad[5:6, :LANES],
-                quad[5:6, LANES:],
-                jnp.broadcast_to(moved[3:4], (1, LANES)),
-                jnp.broadcast_to(moved[4:5], (1, LANES)),
-            ],
-            axis=0,
+            [low[0:1], high[0:1], low[2:3], high[2:3], quad[4:5, :LANES], quad[4:5, LANES:]], axis=0
         )
         tab_x[turn].start()
         tab_all[turn, me_m] = tab_src[turn]
@@ -443,6 +444,8 @@
         total = far_all[turn, 0]
         for k in range(1, n_mp):
             total = total + far_all[turn, k]
+        for p in range(2):
+            cent_ref[p, turn : turn + 1, :] = pltpu.roll(total, LANES - (2 + p) * bunches, 1)[:, :bunches]
         total = jnp.broadcast_to(total, (bunches, LANES))
         far = [
             jnp.sum(jnp.where(full_lane == full_row + p * bunches, total, 0.0), axis=1, keepdims=True)
@@ -456,16 +459,12 @@
         for k in range(6):
             row = column(k)
             rows_ref[k] = row + far[k // 2] if k < 4 else row
-        for p in range(2):
-            spot = jnp.where(full_row == full_lane, column(6 + p), 0.0)
-            cent_ref[p, turn : turn + 1, :] = jnp.sum(spot, axis=0, keepdims=True)[:, :bunches]
 
     def first_sends():
-        pl.semaphore_wait(barrier, n_mp + n_bunch - 2)
         send_sums(0, lane_sums(0), lane_sums(2))
         send_history()
 
-    bin_all(0, first_ids, phase_ref, first_sends)
+    bin_all(0, first_ids, phase_ref, lambda: pl.semaphore_wait(barrier, n_mp + n_bunch - 2), first_sends)
     lay_wake()
 
     loads[5].wait()
@@ -477,8 +476,13 @@
         rot[2 * p] = cos
         rot[2 * p + 1] = sin
 
-    loads[6].wait()
-    loads[7].wait()
+    for k, ref in enumerate((dipole_ref, quad_ref)):
+        loads[6 + k].wait()
+        rest = jnp.transpose(ref[...])
+        for n in range(3):
+            piece = rest.astype(BF16)
+            split[k, n] = piece
+            rest = rest - piece.astype(F32)
     kick_table(0)
     far_first()
     loads[8].wait()
@@ -504,10 +508,9 @@
             return tuple(acc)
 
         zero = jnp.zeros((GROUP, LANES), F32)
-        sums.append(lax.fori_loop(0, parts // WIDTH, kick, (zero, zero), unroll=4))
-    send_sums(1, *(jnp.concatenate([s[p] for s in sums], axis=0) for p in range(2)))
-
-    bin_all(1, next_ids, mid_ref, lambda: None)
+        sums.append(lax.fori_loop(0, parts // WIDTH, kick, (zero, zero), unroll=8))
+    sums = [jnp.concatenate([s[p] for s in sums], axis=0) for p in range(2)]
+    bin_all(1, next_ids, mid_ref, lambda: None, lambda: send_sums(1, *sums))
     kick_table(1)
     far_second()
     lay_rows(1)
@@ -578,18 +581,20 @@
             held(wake_rows, LANES),
             held(SLICES, SLICES),
             held(SLICES, SLICES),
-            held(TURNS, bunches, 8, LANES),
-            held(TURNS, n_mp, 8, LANES),
+            held(TURNS, bunches, 6, LANES),
+            held(TURNS, n_mp, 6, LANES),
             held(8, LANES),
             held(n_bunch, 8, LANES),
             held(TURNS, 2, LANES),
             held(TURNS, n_bunch, 2, LANES),
             held(TURNS, 1, LANES),
             held(TURNS, n_mp, 1, LANES),
-            held(TURNS, 8, LANES),
-            held(TURNS, n_mp, 8, LANES),
+            held(TURNS, 6, LANES),
+            held(TURNS, n_mp, 6, LANES),
             held(TURNS, 2 * bunches, LANES),
             held(4 + turns_back // n_mp, 2, bunches, LANES),
+            held(TURNS, 1, LANES),
+            held(2, 3, SLICES, SLICES, dtype=BF16),
             dma((11,)),
             dma((TURNS,)),
             dma((TURNS,)),

time: 37.9 us -> 36.6 us (0.966)
  Pallas kernels: 37.1 us -> 35.9 us
    pallas_call x1, Pallas kernels: 35.3 us -> 34.1 us  [body(): pl.pallas_call(functools.partial(track_kernel, (n_bunch, n_mp)), out_shap...]
where the time goes in v4:
time: 36.6 us; the launch traced here: 36.5 us
  Pallas kernels  35.9 us (98%)
  between operations  0.64 us (2%)
    pallas_call x1, Pallas kernels, body(): pl.pallas_call(functools.partial(track_kernel, (n_bunch, n_mp)), out_shap...  34.1 us
    pallas_call x1, Pallas kernels, body(): pl.pallas_call(last_kernel, out_shape=(jax.ShapeDtypeStruct(phase_space.s...  1.79 us

profile of v4, /device:TPU:1, one launch (start us, length us, event | category | flops | bytes accessed | tf_op | source)
XLA Modules:
  0.0 36.5 jit_solution(17112916342011002983)
XLA Ops:
  0.6 34.1 %track.1 = (f32[4,16,4096]{2,1,0:T(8,128)S(1)}, s32[16,4096]{1,0:T(8,128)S(1)}, f32[6,16,128]{2,1,0:T(8,128)S(1)}, f32[4,16,128]{2,1,0:T(8,128)S(1)}, f32[2,2,16]{2,1,0:T(2,128)S(1)}) custom-call(f32[4,16,4096]{2,1,0:T(8,128)} %phase_hbm.1, f32[2,16]{1,0:T(2,128)} %advance_hbm.1, f32[2,16,64]{2,1,0:T(8,128)} %bitcast.3, f32[130,128]{1,0:T(8,128)} %bitcast.2, ...), custom_call_target="tpu_custom_call" | custom-call | flops 67108864 | bytes 3145728 | tf_op jit(solution)/shard_map/track/pallas_call | solution.py:565
  34.7 1.8 %last.1 = (f32[4,16,4096]{2,1,0:T(8,128)}, f32[2,2,16]{2,1,0:T(2,128)}) custom-call(f32[4,16,4096]{2,1,0:T(8,128)S(1)} %get-tuple-element.7.mid_ref, s32[16,4096]{1,0:T(8,128)S(1)} %get-tuple-element.8.ids_ref, f32[6,16,128]{2,1,0:T(8,128)S(1)} %get-tuple-element.9.rows_ref, f32[4,16,128]{2,1,0:T(8,128)S(1)} %get-tuple-element.10.rot, ...), custom_call_target="tpu_custom_call" | custom-call | flops 6553600 | bytes 1048576 | tf_op jit(solution)/shard_map/last/pallas_call | solution.py:630

commit v5 on v4

--- a/solution.py
+++ b/solution.py
@@ -14,7 +14,7 @@
 COARSE, FINE = 8, 32
 CHUNK = 512
 GROUP = 8
-AT_ONCE = 8
+BLOCKS = (6, 10)
 WIDTH = 512
 SPANS = 2
 
@@ -108,8 +108,6 @@
     hist_all,
     sum_src,
     sum_all,
-    far_src,
-    far_all,
     tab_src,
     tab_all,
     ext,
@@ -119,12 +117,8 @@
     load,
     msg_send,
     msg_recv,
-    hist_send,
-    hist_recv,
     sum_send,
     sum_recv,
-    far_send,
-    far_recv,
     tab_send,
     tab_recv,
 ):
@@ -134,6 +128,15 @@
     turns_back = hist_ref.shape[2]
     share = turns_back // n_mp
     scale = 1.0 / (parts * n_mp)
+
+    def by_reach(n, step):
+        return sorted(range(1, n), key=lambda k: -min(k // step, (n - k) // step))
+
+    across, along = by_reach(n_bunch, 1), by_reach(n_mp, 2)
+    barrier = pltpu.get_barrier_semaphore()
+    for k, n in zip(along, across):
+        pl.semaphore_signal(barrier, inc=1, device_id={"mp": lax.rem(me_m + k, n_mp)})
+        pl.semaphore_signal(barrier, inc=1, device_id={"bunch": lax.rem(me_b + n, n_bunch)})
 
     loads = [
         pltpu.make_async_copy(source, target, load.at[k])
@@ -156,15 +159,6 @@
     for copy in loads:
         copy.start()
 
-    barrier = pltpu.get_barrier_semaphore()
-    for k in range(1, n_mp):
-        pl.semaphore_signal(barrier, inc=1, device_id={"mp": lax.rem(me_m + k, n_mp)})
-    for k in range(1, n_bunch):
-        pl.semaphore_signal(barrier, inc=1, device_id={"bunch": lax.rem(me_b + k, n_bunch)})
-
-    def by_reach(n, step):
-        return sorted(range(1, n), key=lambda k: -min(k // step, (n - k) // step))
-
     class Exchange:
         def __init__(self, axis, me, offsets, source, target, send, recv):
             self.axis, self.me, self.offsets = axis, me, offsets
@@ -196,15 +190,9 @@
         def leave(self):
             self.all_of_them().wait_send()
 
-    across, along = by_reach(n_bunch, 1), by_reach(n_mp, 2)
-    hist_x = Exchange("bunch", me_b, across, hist_src, hist_all, hist_send, hist_recv)
     sum_x = [
-        Exchange("bunch", me_b, across, sum_src.at[t], sum_all.at[t], sum_send.at[t], sum_recv.at[t])
-        for t in range(TURNS)
-    ]
-    far_x = [
-        Exchange("mp", me_m, along, far_src.at[t], far_all.at[t], far_send.at[t], far_recv.at[t])
-        for t in range(TURNS)
+        Exchange("bunch", me_b, across, source, target, sum_send.at[t], sum_recv.at[t])
+        for t, (source, target) in enumerate(((hist_src, hist_all), (sum_src, sum_all)))
     ]
     tab_x = [
         Exchange("mp", me_m, along, tab_src.at[t], tab_all.at[t], tab_send.at[t], tab_recv.at[t])
@@ -239,16 +227,14 @@
         )
         return jnp.concatenate([rows, jnp.zeros((16, LANES - block.shape[0]), F32)], axis=1)
 
-    def send_sums(turn, sums_x, sums_y):
+    def sum_rows(turn, sums_x, sums_y):
         both = to_lanes(jnp.ones((16, LANES), F32), jnp.concatenate([sums_x, sums_y], axis=0) * scale)[:8]
         partial[turn] = pltpu.roll(both, 2 * bunches, 1)[:1]
         x = pltpu.roll(jnp.where(lane8 < bunches, both, 0.0), place, 1)
         y = jnp.where((lane8 >= bunches) & (lane8 < 2 * bunches), both, 0.0)
         y = pltpu.roll(y, lax.rem(place + LANES - bunches, LANES), 1)
         rows = jnp.where(row8 == 0, x, y)[:2]
-        sum_src[turn] = rows
-        sum_all[turn, me_b] = rows
-        sum_x[turn].start()
+        return rows
 
     def lane_sums(p):
         def step(c, acc):
@@ -256,18 +242,17 @@
 
         return lax.fori_loop(0, parts // LANES, step, jnp.zeros((bunches, LANES), F32), unroll=8)
 
-    def send_history():
-        loads[3].wait()
-        r, c = iota((16, 2 * turns_back), 0), iota((16, 2 * turns_back), 1)
-        chosen = jnp.where(c == (r // share) * turns_back + me_m * share + (r & (share - 1)), 1.0, 0.0)
-        own = to_lanes(chosen, jnp.concatenate([hist_ref[0], hist_ref[1]], axis=1))[:8]
-        own = pltpu.roll(own, place, 1)
-        hist_src[...] = own
-        hist_all[me_b] = own
-        hist_x.start()
+    loads[3].wait()
+    r, c = iota((16, 2 * turns_back), 0), iota((16, 2 * turns_back), 1)
+    chosen = jnp.where(c == (r // share) * turns_back + me_m * share + (r & (share - 1)), 1.0, 0.0)
+    own = to_lanes(chosen, jnp.concatenate([hist_ref[0], hist_ref[1]], axis=1))[: 2 * share]
+    own = pltpu.roll(own, place, 1)
 
     loads[0].wait()
     loads[1].wait()
+    own = jnp.concatenate([own, sum_rows(0, lane_sums(0), lane_sums(2))], axis=0)
+    hist_src[...] = own
+    hist_all[me_b] = own
     loads[2].wait()
 
     iota_c = iota((COARSE, CHUNK), 0)
@@ -309,21 +294,19 @@
         there = lax.rem(chip + reach + chips, chips)
         return there * 2 + lax.rem(core + 1 + side, 2)
 
-    def bin_all(turn, ids_ref, source, before, after):
-        for first in range(0, bunches, AT_ONCE):
-            owners = [owner(first + k) for k in range(AT_ONCE)]
-            tiles = [as_tile(bin_bunch(ids_ref, source, b)) for b in owners]
-            if first == 0:
-                before()
-            if first + AT_ONCE == bunches:
-                landed[turn, me_m] = tiles[-1]
-                owners = owners[:-1]
-            for b, tile in zip(owners, tiles):
-                msg[turn, b] = tile
-            for b in owners:
-                send_msg(turn, b)
-            if first == 0:
-                after()
+    def bin_block(turn, ids_ref, source, first, count):
+        owners = [owner(first + k) for k in range(count)]
+        tiles = [as_tile(bin_bunch(ids_ref, source, b)) for b in owners]
+        if first + count == bunches:
+            landed[turn, me_m] = tiles[-1]
+            owners = owners[:-1]
+        for b, tile in zip(owners, tiles):
+            msg[turn, b] = tile
+        return owners
+
+    def send_all(turn, owners):
+        for b in owners:
+            send_msg(turn, b)
 
     def toeplitz_rows(r, half, sub):
         d = me_b * bunches + sub * 8 + row8 - (LANES * half + lane8) - 1
@@ -345,11 +328,8 @@
     def row_of(tile, k):
         return jnp.broadcast_to(tile[k : k + 1, :], (8, LANES))
 
-    def send_far(turn):
-        row = to_lanes(jnp.ones((16, LANES), F32), ext[turn])[:1] + partial[turn]
-        far_src[turn] = row
-        far_all[turn, me_m] = row
-        far_x[turn].start()
+    def far_row(turn):
+        return to_lanes(jnp.ones((16, LANES), F32), ext[turn])[:1] + partial[turn]
 
     def lay_wake():
         loads[4].wait()
@@ -373,15 +353,14 @@
 
     def far_first():
         sum_x[0].arrive()
-        hist_x.arrive()
-        hist, cent = collected(hist_all), collected(sum_all.at[0])
+        hist = cent = collected(hist_all)
         for sub in range(2):
             at = pl.ds(8 * sub, 8)
             sums = [[jnp.zeros((8, LANES), F32) for _ in range(2)] for _ in range(2)]
             for half in range(2):
                 u = [toep[k, half, at, :] for k in range(share + 4)]
                 for p in range(2):
-                    c = row_of(cent[half], p)
+                    c = row_of(cent[half], 2 * share + p)
                     sums[0][p] = sums[0][p] + u[0] * c
                     sums[1][p] = sums[1][p] + u[1] * c
                 for k in range(share):
@@ -393,11 +372,11 @@
             for turn in range(2):
                 for p in range(2):
                     ext[turn, pl.ds(p * bunches + 8 * sub, 8), :] = sums[turn][p]
-        send_far(0)
+        tab_src[0, 6:7, :] = far_row(0)
 
     def far_second():
         sum_x[1].arrive()
-        cent = collected(sum_all.at[1])
+        cent = collected(sum_all)
         for sub in range(2):
             for p in range(2):
                 at = pl.ds(p * bunches + 8 * sub, 8)
@@ -405,7 +384,7 @@
                 for half in range(2):
                     total = total + toep[0, half, pl.ds(8 * sub, 8), :] * row_of(cent[half], p)
                 ext[1, at, :] = total
-        send_far(1)
+        tab_src[1, 6:7, :] = far_row(1)
 
     def kick_table(turn):
         msg_x[turn].arrive()
@@ -431,7 +410,7 @@
 
         dip, quad = product(0), product(1)
         low, high = dip[:, :LANES], dip[:, LANES:]
-        tab_src[turn] = jnp.concatenate(
+        tab_src[turn, :6, :] = jnp.concatenate(
             [low[0:1], high[0:1], low[2:3], high[2:3], quad[4:5, :LANES], quad[4:5, LANES:]], axis=0
         )
         tab_x[turn].start()
@@ -440,10 +419,10 @@
     full_row, full_lane = iota((bunches, LANES), 0), iota((bunches, LANES), 1)
 
     def lay_rows(turn):
-        far_x[turn].arrive()
-        total = far_all[turn, 0]
+        tab_x[turn].arrive()
+        total = tab_all[turn, 0, 6:7, :]
         for k in range(1, n_mp):
-            total = total + far_all[turn, k]
+            total = total + tab_all[turn, k, 6:7, :]
         for p in range(2):
             cent_ref[p, turn : turn + 1, :] = pltpu.roll(total, LANES - (2 + p) * bunches, 1)[:, :bunches]
         total = jnp.broadcast_to(total, (bunches, LANES))
@@ -451,7 +430,6 @@
             jnp.sum(jnp.where(full_lane == full_row + p * bunches, total, 0.0), axis=1, keepdims=True)
             for p in range(2)
         ]
-        tab_x[turn].arrive()
 
         def column(k):
             return jnp.concatenate([tab_all[turn, n, k : k + 1, :] for n in range(bunches)], axis=0)
@@ -460,11 +438,12 @@
             row = column(k)
             rows_ref[k] = row + far[k // 2] if k < 4 else row
 
-    def first_sends():
-        send_sums(0, lane_sums(0), lane_sums(2))
-        send_history()
-
-    bin_all(0, first_ids, phase_ref, lambda: pl.semaphore_wait(barrier, n_mp + n_bunch - 2), first_sends)
+    half = bunches // 2
+    owners = bin_block(0, first_ids, phase_ref, 0, half) + bin_block(0, first_ids, phase_ref, half, half)
+    pl.semaphore_wait(barrier, n_mp + n_bunch - 2)
+    send_all(0, owners[:half])
+    sum_x[0].start()
+    send_all(0, owners[half:])
     lay_wake()
 
     loads[5].wait()
@@ -483,8 +462,8 @@
             piece = rest.astype(BF16)
             split[k, n] = piece
             rest = rest - piece.astype(F32)
+    far_first()
     kick_table(0)
-    far_first()
     loads[8].wait()
     loads[9].wait()
     loads[10].wait()
@@ -510,15 +489,21 @@
         zero = jnp.zeros((GROUP, LANES), F32)
         sums.append(lax.fori_loop(0, parts // WIDTH, kick, (zero, zero), unroll=8))
     sums = [jnp.concatenate([s[p] for s in sums], axis=0) for p in range(2)]
-    bin_all(1, next_ids, mid_ref, lambda: None, lambda: send_sums(1, *sums))
+    rows = sum_rows(1, *sums)
+    sum_src[...] = rows
+    sum_all[me_b] = rows
+    sum_x[1].start()
+    first = 0
+    for count in BLOCKS:
+        send_all(1, bin_block(1, next_ids, mid_ref, first, count))
+        first += count
+    far_second()
     kick_table(1)
-    far_second()
     lay_rows(1)
 
     for turn in range(TURNS):
-        for exchange in (msg_x[turn], tab_x[turn], far_x[turn], sum_x[turn]):
+        for exchange in (msg_x[turn], tab_x[turn], sum_x[turn]):
             exchange.leave()
-    hist_x.leave()
 
 
 def last_kernel(mid_ref, ids_ref, rows_ref, rot, cent_in, out_hbm, cent_hbm, out_ref, cent_ref, sems):
@@ -583,23 +568,17 @@
             held(SLICES, SLICES),
             held(TURNS, bunches, 6, LANES),
             held(TURNS, n_mp, 6, LANES),
-            held(8, LANES),
-            held(n_bunch, 8, LANES),
-            held(TURNS, 2, LANES),
-            held(TURNS, n_bunch, 2, LANES),
-            held(TURNS, 1, LANES),
-            held(TURNS, n_mp, 1, LANES),
-            held(TURNS, 6, LANES),
-            held(TURNS, n_mp, 6, LANES),
+            held(2 + 2 * turns_back // n_mp, LANES),
+            held(n_bunch, 2 + 2 * turns_back // n_mp, LANES),
+            held(2, LANES),
+            held(n_bunch, 2, LANES),
+            held(TURNS, 7, LANES),
+            held(TURNS, n_mp, 7, LANES),
             held(TURNS, 2 * bunches, LANES),
             held(4 + turns_back // n_mp, 2, bunches, LANES),
             held(TURNS, 1, LANES),
             held(2, 3, SLICES, SLICES, dtype=BF16),
             dma((11,)),
-            dma((TURNS,)),
-            dma((TURNS,)),
-            dma,
-            dma,
             dma((TURNS,)),
             dma((TURNS,)),
             dma((TURNS,)),

time: 36.6 us -> 36.9 us (level)
  no operation moved by 1% of the time
where the time goes in v5:
time: 36.9 us; the launch traced here: 36.8 us
  Pallas kernels  36.1 us (98%)
  between operations  0.64 us (2%)
    pallas_call x1, Pallas kernels, body(): pl.pallas_call(functools.partial(track_kernel, (n_bunch, n_mp)), out_shap...  34.4 us
    pallas_call x1, Pallas kernels, body(): pl.pallas_call(last_kernel, out_shape=(jax.ShapeDtypeStruct(phase_space.s...  1.79 us

profile of v5, /device:TPU:1, one launch (start us, length us, event | category | flops | bytes accessed | tf_op | source)
XLA Modules:
  0.0 36.8 jit_solution(15804112025361255912)
XLA Ops:
  0.6 34.4 %track.1 = (f32[4,16,4096]{2,1,0:T(8,128)S(1)}, s32[16,4096]{1,0:T(8,128)S(1)}, f32[6,16,128]{2,1,0:T(8,128)S(1)}, f32[4,16,128]{2,1,0:T(8,128)S(1)}, f32[2,2,16]{2,1,0:T(2,128)S(1)}) custom-call(f32[4,16,4096]{2,1,0:T(8,128)} %phase_hbm.1, f32[2,16]{1,0:T(2,128)} %advance_hbm.1, f32[2,16,64]{2,1,0:T(8,128)} %bitcast.3, f32[130,128]{1,0:T(8,128)} %bitcast.2, ...), custom_call_target="tpu_custom_call" | custom-call | flops 67108864 | bytes 3145728 | tf_op jit(solution)/shard_map/track/pallas_call | solution.py:550
  35.0 1.8 %last.1 = (f32[4,16,4096]{2,1,0:T(8,128)}, f32[2,2,16]{2,1,0:T(2,128)}) custom-call(f32[4,16,4096]{2,1,0:T(8,128)S(1)} %get-tuple-element.7.mid_ref, s32[16,4096]{1,0:T(8,128)S(1)} %get-tuple-element.8.ids_ref, f32[6,16,128]{2,1,0:T(8,128)S(1)} %get-tuple-element.9.rows_ref, f32[4,16,128]{2,1,0:T(8,128)S(1)} %get-tuple-element.10.rot, ...), custom_call_target="tpu_custom_call" | custom-call | flops 6553600 | bytes 1048576 | tf_op jit(solution)/shard_map/last/pallas_call | solution.py:609

commit v6 on v5

--- a/solution.py
+++ b/solution.py
@@ -14,7 +14,7 @@
 COARSE, FINE = 8, 32
 CHUNK = 512
 GROUP = 8
-BLOCKS = (6, 10)
+BLOCKS = (8, 8)
 WIDTH = 512
 SPANS = 2
 
@@ -250,9 +250,6 @@
 
     loads[0].wait()
     loads[1].wait()
-    own = jnp.concatenate([own, sum_rows(0, lane_sums(0), lane_sums(2))], axis=0)
-    hist_src[...] = own
-    hist_all[me_b] = own
     loads[2].wait()
 
     iota_c = iota((COARSE, CHUNK), 0)
@@ -353,26 +350,30 @@
 
     def far_first():
         sum_x[0].arrive()
-        hist = cent = collected(hist_all)
+        tiles = collected(hist_all)
         for sub in range(2):
             at = pl.ds(8 * sub, 8)
-            sums = [[jnp.zeros((8, LANES), F32) for _ in range(2)] for _ in range(2)]
-            for half in range(2):
-                u = [toep[k, half, at, :] for k in range(share + 4)]
-                for p in range(2):
-                    c = row_of(cent[half], 2 * share + p)
-                    sums[0][p] = sums[0][p] + u[0] * c
-                    sums[1][p] = sums[1][p] + u[1] * c
-                for k in range(share):
-                    for p in range(2):
-                        h = row_of(hist[half], p * share + k)
-                        sums[0][p] = sums[0][p] + u[2 + k] * h
-                        later = u[3 + k] if k < share - 1 else u[3 + share]
-                        sums[1][p] = sums[1][p] + later * h
-            for turn in range(2):
-                for p in range(2):
-                    ext[turn, pl.ds(p * bunches + 8 * sub, 8), :] = sums[turn][p]
+            for p in range(2):
+                total = jnp.zeros((8, LANES), F32)
+                for half in range(2):
+                    total = total + toep[0, half, at, :] * row_of(tiles[half], 2 * share + p)
+                    for k in range(share):
+                        total = total + toep[2 + k, half, at, :] * row_of(tiles[half], p * share + k)
+                ext[0, pl.ds(p * bunches + 8 * sub, 8), :] = total
         tab_src[0, 6:7, :] = far_row(0)
+        return tiles
+
+    def far_later(tiles):
+        for sub in range(2):
+            at = pl.ds(8 * sub, 8)
+            for p in range(2):
+                total = jnp.zeros((8, LANES), F32)
+                for half in range(2):
+                    total = total + toep[1, half, at, :] * row_of(tiles[half], 2 * share + p)
+                    for k in range(share):
+                        later = toep[3 + k if k < share - 1 else 3 + share, half, at, :]
+                        total = total + later * row_of(tiles[half], p * share + k)
+                ext[1, pl.ds(p * bunches + 8 * sub, 8), :] = total
 
     def far_second():
         sum_x[1].arrive()
@@ -439,7 +440,12 @@
             rows_ref[k] = row + far[k // 2] if k < 4 else row
 
     half = bunches // 2
-    owners = bin_block(0, first_ids, phase_ref, 0, half) + bin_block(0, first_ids, phase_ref, half, half)
+    first_sums = (lane_sums(0), lane_sums(2))
+    owners = bin_block(0, first_ids, phase_ref, 0, half)
+    own = jnp.concatenate([own, sum_rows(0, *first_sums)], axis=0)
+    hist_src[...] = own
+    hist_all[me_b] = own
+    owners = owners + bin_block(0, first_ids, phase_ref, half, half)
     pl.semaphore_wait(barrier, n_mp + n_bunch - 2)
     send_all(0, owners[:half])
     sum_x[0].start()
@@ -462,8 +468,9 @@
             piece = rest.astype(BF16)
             split[k, n] = piece
             rest = rest - piece.astype(F32)
-    far_first()
+    tiles = far_first()
     kick_table(0)
+    far_later(tiles)
     loads[8].wait()
     loads[9].wait()
     loads[10].wait()

time: 36.9 us -> 36.4 us (0.986)
  Pallas kernels: 36.1 us -> 35.7 us
    pallas_call x1, Pallas kernels: 34.4 us -> 33.9 us  [body(): pl.pallas_call(functools.partial(track_kernel, (n_bunch, n_mp)), out_shap...]
where the time goes in v6:
time: 36.4 us; the launch traced here: 36.3 us
  Pallas kernels  35.7 us (98%)
  between operations  0.64 us (2%)
    pallas_call x1, Pallas kernels, body(): pl.pallas_call(functools.partial(track_kernel, (n_bunch, n_mp)), out_shap...  33.9 us
    pallas_call x1, Pallas kernels, body(): pl.pallas_call(last_kernel, out_shape=(jax.ShapeDtypeStruct(phase_space.s...  1.79 us

profile of v6, /device:TPU:1, one launch (start us, length us, event | category | flops | bytes accessed | tf_op | source)
XLA Modules:
  0.0 36.3 jit_solution(2603449893125427835)
XLA Ops:
  0.6 33.9 %track.1 = (f32[4,16,4096]{2,1,0:T(8,128)S(1)}, s32[16,4096]{1,0:T(8,128)S(1)}, f32[6,16,128]{2,1,0:T(8,128)S(1)}, f32[4,16,128]{2,1,0:T(8,128)S(1)}, f32[2,2,16]{2,1,0:T(2,128)S(1)}) custom-call(f32[4,16,4096]{2,1,0:T(8,128)} %phase_hbm.1, f32[2,16]{1,0:T(2,128)} %advance_hbm.1, f32[2,16,64]{2,1,0:T(8,128)} %bitcast.3, f32[130,128]{1,0:T(8,128)} %bitcast.2, ...), custom_call_target="tpu_custom_call" | custom-call | flops 67108864 | bytes 3145728 | tf_op jit(solution)/shard_map/track/pallas_call | solution.py:557
  34.5 1.8 %last.1 = (f32[4,16,4096]{2,1,0:T(8,128)}, f32[2,2,16]{2,1,0:T(2,128)}) custom-call(f32[4,16,4096]{2,1,0:T(8,128)S(1)} %get-tuple-element.7.mid_ref, s32[16,4096]{1,0:T(8,128)S(1)} %get-tuple-element.8.ids_ref, f32[6,16,128]{2,1,0:T(8,128)S(1)} %get-tuple-element.9.rows_ref, f32[4,16,128]{2,1,0:T(8,128)S(1)} %get-tuple-element.10.rot, ...), custom_call_target="tpu_custom_call" | custom-call | flops 6553600 | bytes 1048576 | tf_op jit(solution)/shard_map/last/pallas_call | solution.py:616

commit v7 on v6

--- a/solution.py
+++ b/solution.py
@@ -133,11 +133,6 @@
         return sorted(range(1, n), key=lambda k: -min(k // step, (n - k) // step))
 
     across, along = by_reach(n_bunch, 1), by_reach(n_mp, 2)
-    barrier = pltpu.get_barrier_semaphore()
-    for k, n in zip(along, across):
-        pl.semaphore_signal(barrier, inc=1, device_id={"mp": lax.rem(me_m + k, n_mp)})
-        pl.semaphore_signal(barrier, inc=1, device_id={"bunch": lax.rem(me_b + n, n_bunch)})
-
     loads = [
         pltpu.make_async_copy(source, target, load.at[k])
         for k, (source, target) in enumerate(
@@ -156,7 +151,15 @@
             )
         )
     ]
-    for copy in loads:
+    for copy in loads[:4]:
+        copy.start()
+
+    barrier = pltpu.get_barrier_semaphore()
+    for k, n in zip(along, across):
+        pl.semaphore_signal(barrier, inc=1, device_id={"mp": lax.rem(me_m + k, n_mp)})
+        pl.semaphore_signal(barrier, inc=1, device_id={"bunch": lax.rem(me_b + n, n_bunch)})
+
+    for copy in loads[4:]:
         copy.start()
 
     class Exchange:

time: 36.4 us -> 36.2 us (level)
  no operation moved by 1% of the time
where the time goes in v7:
time: 36.2 us; the launch traced here: 36.1 us
  Pallas kernels  35.5 us (98%)
  between operations  0.64 us (2%)
    pallas_call x1, Pallas kernels, body(): pl.pallas_call(functools.partial(track_kernel, (n_bunch, n_mp)), out_shap...  33.7 us
    pallas_call x1, Pallas kernels, body(): pl.pallas_call(last_kernel, out_shape=(jax.ShapeDtypeStruct(phase_space.s...  1.79 us

profile of v7, /device:TPU:1, one launch (start us, length us, event | category | flops | bytes accessed | tf_op | source)
XLA Modules:
  0.0 36.1 jit_solution(10064141228059692094)
XLA Ops:
  0.6 33.7 %track.1 = (f32[4,16,4096]{2,1,0:T(8,128)S(1)}, s32[16,4096]{1,0:T(8,128)S(1)}, f32[6,16,128]{2,1,0:T(8,128)S(1)}, f32[4,16,128]{2,1,0:T(8,128)S(1)}, f32[2,2,16]{2,1,0:T(2,128)S(1)}) custom-call(f32[4,16,4096]{2,1,0:T(8,128)} %phase_hbm.1, f32[2,16]{1,0:T(2,128)} %advance_hbm.1, f32[2,16,64]{2,1,0:T(8,128)} %bitcast.3, f32[130,128]{1,0:T(8,128)} %bitcast.2, ...), custom_call_target="tpu_custom_call" | custom-call | flops 67108864 | bytes 3145728 | tf_op jit(solution)/shard_map/track/pallas_call | solution.py:560
  34.3 1.8 %last.1 = (f32[4,16,4096]{2,1,0:T(8,128)}, f32[2,2,16]{2,1,0:T(2,128)}) custom-call(f32[4,16,4096]{2,1,0:T(8,128)S(1)} %get-tuple-element.7.mid_ref, s32[16,4096]{1,0:T(8,128)S(1)} %get-tuple-element.8.ids_ref, f32[6,16,128]{2,1,0:T(8,128)S(1)} %get-tuple-element.9.rows_ref, f32[4,16,128]{2,1,0:T(8,128)S(1)} %get-tuple-element.10.rot, ...), custom_call_target="tpu_custom_call" | custom-call | flops 6553600 | bytes 1048576 | tf_op jit(solution)/shard_map/last/pallas_call | solution.py:619

commit v8 on v7

--- a/solution.py
+++ b/solution.py
@@ -29,6 +29,12 @@
 
 def gather_lanes(row, index):
     return jnp.take_along_axis(row, index, axis=1, mode="promise_in_bounds")
+
+
+def added(terms):
+    while len(terms) > 1:
+        terms = [sum(terms[k + 1 : k + 2], terms[k]) for k in range(0, len(terms), 2)]
+    return terms[0]
 
 
 def two_pieces(v):
@@ -392,9 +398,7 @@
 
     def kick_table(turn):
         msg_x[turn].arrive()
-        total = landed[turn, 0]
-        for k in range(1, 16):
-            total = total + landed[turn, k]
+        total = added([landed[turn, k] for k in range(n_mp)])
         total = jnp.concatenate([total, jnp.zeros((2, LANES), F32)], axis=0)
         wide = jnp.concatenate([total, pltpu.roll(total, 7, 0)], axis=1)
         stack = []
@@ -424,9 +428,7 @@
 
     def lay_rows(turn):
         tab_x[turn].arrive()
-        total = tab_all[turn, 0, 6:7, :]
-        for k in range(1, n_mp):
-            total = total + tab_all[turn, k, 6:7, :]
+        total = added([tab_all[turn, k, 6:7, :] for k in range(n_mp)])
         for p in range(2):
             cent_ref[p, turn : turn + 1, :] = pltpu.roll(total, LANES - (2 + p) * bunches, 1)[:, :bunches]
         total = jnp.broadcast_to(total, (bunches, LANES))

time: 36.2 us -> 36.2 us (level)
  no operation moved by 1% of the time
where the time goes in v8:
time: 36.2 us; the launch traced here: 36.1 us
  Pallas kernels  35.4 us (98%)
  between operations  0.64 us (2%)
    pallas_call x1, Pallas kernels, body(): pl.pallas_call(functools.partial(track_kernel, (n_bunch, n_mp)), out_shap...  33.6 us
    pallas_call x1, Pallas kernels, body(): pl.pallas_call(last_kernel, out_shape=(jax.ShapeDtypeStruct(phase_space.s...  1.79 us

profile of v8, /device:TPU:1, one launch (start us, length us, event | category | flops | bytes accessed | tf_op | source)
XLA Modules:
  0.0 36.1 jit_solution(3170053951449389137)
XLA Ops:
  0.6 33.6 %track.1 = (f32[4,16,4096]{2,1,0:T(8,128)S(1)}, s32[16,4096]{1,0:T(8,128)S(1)}, f32[6,16,128]{2,1,0:T(8,128)S(1)}, f32[4,16,128]{2,1,0:T(8,128)S(1)}, f32[2,2,16]{2,1,0:T(2,128)S(1)}) custom-call(f32[4,16,4096]{2,1,0:T(8,128)} %phase_hbm.1, f32[2,16]{1,0:T(2,128)} %advance_hbm.1, f32[2,16,64]{2,1,0:T(8,128)} %bitcast.3, f32[130,128]{1,0:T(8,128)} %bitcast.2, ...), custom_call_target="tpu_custom_call" | custom-call | flops 67108864 | bytes 3145728 | tf_op jit(solution)/shard_map/track/pallas_call | solution.py:562
  34.3 1.8 %last.1 = (f32[4,16,4096]{2,1,0:T(8,128)}, f32[2,2,16]{2,1,0:T(2,128)}) custom-call(f32[4,16,4096]{2,1,0:T(8,128)S(1)} %get-tuple-element.7.mid_ref, s32[16,4096]{1,0:T(8,128)S(1)} %get-tuple-element.8.ids_ref, f32[6,16,128]{2,1,0:T(8,128)S(1)} %get-tuple-element.9.rows_ref, f32[4,16,128]{2,1,0:T(8,128)S(1)} %get-tuple-element.10.rot, ...), custom_call_target="tpu_custom_call" | custom-call | flops 6553600 | bytes 1048576 | tf_op jit(solution)/shard_map/last/pallas_call | solution.py:621
